TPU v7x, 32 devices: a whole 2x2x4 slice. The times are simulated.
32 devices in a mesh: vec: 8 (over z, y), grid: 4 (over x, core).
Axes of the slice: x: 2, y: 2, z: 4, core: 2. Of those that a mesh axis runs over, the one named last changes fastest.
Arguments:
- fitting_vectors: float32 [32, 32, 1024], P('vec', 'grid'), may hold values from -6 to 6
Outputs:
- coulomb_blocks: float32 [32, 5, 4], P(('vec', 'grid'))
All inputs are finite; a program needn't handle non-finite values.
Results may differ from a plain program's by a relative error of at most 0.00005.
Values sent between devices are 32-bit elements; how exact they have to be, the bound alone decides.
No kernel may reach another device: no remote copies, remote signals or barrier semaphores. Data moves between devices by JAX's collectives and lax.ppermute only.
A program may use at most 64 MiB of HBM per device.

v0:
```python
import functools
import math

import jax
import jax.numpy as jnp
import numpy as np
from jax import lax
from jax.experimental import pallas as pl
from jax.experimental.pallas import tpu as pltpu
from jax.sharding import PartitionSpec as P

AXES = ("vec", "grid")
LANES = 128
ROWS = 8


def centred(size):
    return np.arange(size) - (size - 1) / 2


def pair_table(size):
    omega = math.pi / size
    freqs = np.arange(size)
    cosines = np.cos(omega * np.outer(freqs, centred(size)))
    sines = np.sin(omega * np.outer(np.where(freqs == 0, size, freqs), centred(size)))
    return np.stack([cosines, sines], 1).astype(np.float32)


def multiplicity(size):
    return np.where(np.isin(np.arange(size + 1), (0, size)), 1.0, 2.0)


def operator_spectrum(size, pair, kx_pad=0, ky_pad=0):
    kz = jnp.stack([pair, jnp.where(pair == 0, size, pair)]).astype(jnp.float32)
    times = jnp.where(pair == 0, 1.0, 2.0)
    ky = jnp.arange(size + 1 + ky_pad, dtype=jnp.int32)
    kx = jnp.arange(size + 1 + kx_pad, dtype=jnp.int32)
    fy, fx = ky.astype(jnp.float32), kx.astype(jnp.float32)
    total_sq = (kz * kz)[:, None, None] + (fy * fy)[None, :, None] + (fx * fx)[None, None, :]
    wave_sq = total_sq * (math.pi / size) ** 2
    safe_sq = jnp.where(total_sq > 0, wave_sq, 1.0)
    half_arg = 0.5 * jnp.sqrt(safe_sq) * size
    values = 8.0 * math.pi * jnp.sin(half_arg) ** 2 / safe_sq
    values = jnp.where(total_sq > 0, values, 2.0 * math.pi * size * size)

    def weight(k):
        inside = jnp.where((k == 0) | (k == size), 1.0, 2.0)
        return jnp.where(k <= size, inside, 0.0)

    scale = times / (float(2 * size) ** 3 * float(size) ** 3)
    return values * weight(ky)[None, :, None] * weight(kx)[None, None, :] * scale


def split_bf16(value):
    high = value.astype(jnp.bfloat16)
    return high, (value - high.astype(jnp.float32)).astype(jnp.bfloat16)


def split_table(table):
    table = np.asarray(table, np.float32)
    high = table.astype(jnp.bfloat16)
    return high, (table - high.astype(np.float32)).astype(jnp.bfloat16)


def analyse_kernel(size, n_grid, field_ref, table_ref, out_ref, held_ref):
    group, slab, _ = field_ref.shape
    half = size // 2
    per_block = LANES // size
    blocks = size // per_block
    lane_group = lax.broadcasted_iota(jnp.int32, (blocks * slab, LANES), 1) // size
    stacked = [
        jnp.concatenate([field_ref[v, :, b * LANES : (b + 1) * LANES] for b in range(blocks)], 0)
        for v in range(group)
    ]
    turned = []
    for q in range(per_block):
        mixed = None
        for v in range(group):
            shift = (v - q) % per_block * size
            part = pltpu.roll(stacked[v], shift, 1) if shift else stacked[v]
            mixed = part if mixed is None else jnp.where(lane_group == v, part, mixed)
        turned.append(mixed)
    for y in range(half):
        b, q = divmod(y, per_block)
        other_b, other_q = divmod(size - 1 - y, per_block)
        near = turned[q][b * slab : (b + 1) * slab]
        far = turned[other_q][other_b * slab : (other_b + 1) * slab]
        held_ref[0, y * slab : (y + 1) * slab, :] = near + far
        held_ref[1, y * slab : (y + 1) * slab, :] = near - far
    mirrored = lax.axis_index("grid") >= n_grid // 2
    for parity in range(2):
        rows = []
        for j in range(slab):
            start = jnp.where(mirrored, slab - 1 - j, j)
            rows.append(held_ref[parity, pl.ds(start, half, stride=slab), :])
        high, low = split_bf16(jnp.concatenate(rows, 0))
        operand = jnp.concatenate([high, high, low], 1)
        out_ref[:, parity * LANES : (parity + 1) * LANES] = lax.dot_general(
            table_ref[...], operand, (((1,), (1,)), ((), ())), preferred_element_type=jnp.float32
        )


def operator_kernel(size, spectrum_ref, cos_ref, wave_ref, turn_ref, high_ref, low_ref):
    half = size // 2
    width = half * half
    exact = lax.Precision.HIGHEST
    for c in range(2):
        along = jnp.dot(
            spectrum_ref[c], cos_ref[...], precision=exact, preferred_element_type=jnp.float32
        )
        for parity in range(2):
            strip = jnp.dot(
                turn_ref[parity],
                along * wave_ref[parity],
                precision=exact,
                preferred_element_type=jnp.float32,
            )

            def window(start):
                base = start // LANES * LANES
                part = strip[:, base : base + width + LANES]
                if start > base:
                    part = pltpu.roll(part, part.shape[1] - (start - base), 1)
                return part[:, :width]

            for x in range(half):
                toeplitz = window((size - 1 - x) * half)
                hankel = window(x * half)
                for sign in range(2):
                    value = 0.5 * (toeplitz - hankel if sign else toeplitz + hankel)
                    high, low = split_bf16(value)
                    high_ref[c, parity, sign, x * half : (x + 1) * half, :] = high
                    low_ref[c, parity, sign, x * half : (x + 1) * half, :] = low


def gram_kernel(n_vec, n_grid, group, got_ref, high_ref, low_ref, out_ref):
    per_tile = ROWS // group
    total = n_vec * group
    row = lax.broadcasted_iota(jnp.int32, (ROWS, got_ref.shape[2]), 0)
    left, right = [], []
    for c in range(2):
        slabs = []
        for i in range(n_grid):
            tiles = []
            for g in range(0, n_vec, 2):
                first = got_ref[g * n_grid + i]
                second = got_ref[(g + 1) * n_grid + i]
                if c == 0:
                    second = pltpu.roll(second, group, 0)
                else:
                    first = pltpu.roll(first, group, 0)
                tiles.append(jnp.where(row < group, first, second))
            slabs.append(jnp.concatenate(tiles, 0))
        for sign in range(2):
            folded = []
            for i in range(n_grid // 2):
                near, far = slabs[i], slabs[n_grid - 1 - i]
                folded.append(near - far if sign else near + far)
            for parity in range(2):
                lanes = folded[0].shape[1] // 2
                value = jnp.concatenate(
                    [f[:, parity * lanes : (parity + 1) * lanes] for f in folded], 1
                )
                high, low = split_bf16(value)
                op_high, op_low = high_ref[c, parity, sign], low_ref[c, parity, sign]
                both = jnp.dot(
                    jnp.concatenate([high, low], 0), op_high, preferred_element_type=jnp.float32
                )
                applied = both[:total] + both[total:]
                applied += jnp.dot(high, op_low, preferred_element_type=jnp.float32)
                applied_high, applied_low = split_bf16(applied)
                left += [applied_high, applied_low, applied_high]
                right += [high, high, low]
    copies = LANES // total
    gram = lax.dot_general(
        jnp.concatenate(left, 1),
        jnp.concatenate([jnp.concatenate(right, 1)] * copies, 0),
        (((1,), (1,)), ((), ())),
        preferred_element_type=jnp.float32,
    )
    owner = lax.broadcasted_iota(jnp.int32, gram.shape, 0) // group
    turned = gram
    for g in range(1, n_vec):
        turned = jnp.where(owner == g, pltpu.roll(gram, LANES - g * group, 1), turned)
    out_ref[...] = turned


def finish_kernel(got_ref, out_ref):
    _, shifts, width = out_ref.shape
    summed = jnp.sum(got_ref[...], 0, keepdims=True)
    for s in range(shifts):
        out_ref[0, s : s + 1, :] = summed[:, s * width : (s + 1) * width]


def whole_blocks(count):
    return [pl.BlockSpec(memory_space=pltpu.VMEM)] * count


def tiled_program(fitting_vectors, size, n_vec, n_grid, shifts):
    group, slab, _ = fitting_vectors.shape
    half = size // 2
    n_devices = n_vec * n_grid
    total = n_vec * group
    pair = lax.axis_index(AXES)

    spread = np.einsum("kcz,vw->kcvwz", pair_table(size), np.eye(group))
    high, low = split_table(spread.reshape(size * 2 * group, group * size))
    table = jnp.asarray(np.concatenate([high, low, high], 1))
    components = pl.pallas_call(
        functools.partial(analyse_kernel, size, n_grid),
        out_shape=jax.ShapeDtypeStruct((size * 2 * group, size * slab), jnp.float32),
        in_specs=whole_blocks(2),
        out_specs=whole_blocks(1)[0],
        scratch_shapes=[pltpu.VMEM((2, half * slab, LANES), jnp.float32)],
        name="analyse",
    )(fitting_vectors, table)
    chunks = components.reshape(n_devices, 2 * group, size * slab)
    got = lax.all_to_all(chunks, AXES, 0, 0, tiled=True)

    omega = math.pi / size
    ky_pad = -(size + 1) % ROWS
    kx_pad = -(size + 1) % LANES
    spectrum = operator_spectrum(size, pair, kx_pad, ky_pad)
    freqs_y = np.arange(size + 1 + ky_pad)
    freqs_x = np.arange(size + 1 + kx_pad)
    offsets = np.arange(-(size - 1), size + 1)
    cos_table = np.repeat(np.cos(omega * np.outer(freqs_x, offsets)), half, 1)
    angle = omega * np.outer(freqs_y, centred(size)[:half])
    waves = np.stack([np.cos(angle), np.sin(angle)])
    waves[0, size] = 0.0
    waves[1, 0] = 0.0
    op_shape = jax.ShapeDtypeStruct((2, 2, 2, half * half, half * half), jnp.bfloat16)
    op_high, op_low = pl.pallas_call(
        functools.partial(operator_kernel, size),
        out_shape=(op_shape, op_shape),
        in_specs=whole_blocks(4),
        out_specs=tuple(whole_blocks(2)),
        name="operator",
    )(
        spectrum,
        jnp.asarray(cos_table, jnp.float32),
        jnp.asarray(np.tile(waves, (1, 1, 2 * size)), jnp.float32),
        jnp.asarray(np.swapaxes(waves, 1, 2), jnp.float32),
    )

    rows = pl.pallas_call(
        functools.partial(gram_kernel, n_vec, n_grid, group),
        out_shape=jax.ShapeDtypeStruct((total, LANES), jnp.float32),
        in_specs=whole_blocks(3),
        out_specs=whole_blocks(1)[0],
        name="gram",
    )(got, op_high, op_low)
    parts = lax.all_to_all(rows, AXES, 0, 0, tiled=True)
    return pl.pallas_call(
        finish_kernel,
        out_shape=jax.ShapeDtypeStruct((1, shifts, group), jnp.float32),
        in_specs=whole_blocks(1),
        out_specs=whole_blocks(1)[0],
        name="finish",
    )(parts)


def general_program(fitting_vectors, size, n_vec, n_grid, shifts):
    exact = lax.Precision.HIGHEST
    group, slab, _ = fitting_vectors.shape
    n_devices = n_vec * n_grid
    total = n_vec * group
    rank = lax.axis_index(AXES)
    sharers = max(1, n_devices // size)
    held = max(1, size // n_devices)
    components = jnp.einsum(
        "vxyz,kcz->kcvxy",
        fitting_vectors.reshape(group, slab, size, size),
        jnp.asarray(pair_table(size)),
        precision=exact,
    )
    chunks = jnp.repeat(components, sharers, 0)
    chunks = chunks.reshape(n_devices, held, 2, group, slab, size)
    got = lax.all_to_all(chunks, AXES, 0, 0, tiled=True)
    got = got.reshape(n_vec, n_grid, held, 2, group, slab, size)
    planes = got.transpose(2, 3, 0, 4, 1, 5, 6).reshape(held, 2, total, size * size)

    omega = math.pi / size
    cells = np.arange(size)
    steps = np.cos(
        omega * (cells[:, None, None] - cells[None, :, None]) * np.arange(size + 1)
    ).astype(np.float32)
    columns = size * size // sharers
    start = rank % sharers * columns
    gram = jnp.zeros((total, total), jnp.float32)
    for h in range(held):
        spectrum = operator_spectrum(size, rank // sharers * held + h)
        along = jnp.einsum("clk,xak->clxa", spectrum, steps, precision=exact)
        operator = jnp.einsum("ybl,clxa->cxyab", steps, along, precision=exact)
        operator = operator.reshape(2, size * size, size * size)
        operator = lax.dynamic_slice_in_dim(operator, start, columns, 2)
        applied = jnp.einsum("cmp,cpq->cmq", planes[h], operator, precision=exact)
        own = lax.dynamic_slice_in_dim(planes[h], start, columns, 2)
        gram += jnp.einsum("cmq,cnq->mn", applied, own, precision=exact)
    wanted = (np.arange(n_vec)[:, None] * group + np.arange(shifts * group)) % total
    wanted = np.repeat(wanted, group, 0)
    rows = jnp.take_along_axis(gram, jnp.asarray(wanted), 1)
    rows = rows.reshape(n_devices, total // n_devices, shifts * group)
    parts = lax.all_to_all(rows, AXES, 0, 0, tiled=True)
    return jnp.sum(parts, 0).reshape(total // n_devices, shifts, group)


def body(fitting_vectors):
    n_vec, n_grid = (lax.axis_size(a) for a in AXES)
    group, slab, plane = fitting_vectors.shape
    size = math.isqrt(plane)
    shifts = n_vec // 2 + 1
    tiled = (
        n_vec * n_grid == size
        and group * size == LANES
        and slab * size == 2 * LANES
        and 2 * group == ROWS
        and n_vec * group <= LANES
        and n_vec % 2 == 0
        and n_grid % 2 == 0
        and group == n_grid
    )
    build = tiled_program if tiled else general_program
    return build(fitting_vectors, size, n_vec, n_grid, shifts)


def solution(mesh):
    return jax.shard_map(
        body,
        mesh=mesh,
        in_specs=(P("vec", "grid", None),),
        out_specs=P(("vec", "grid"), None, None),
        check_vma=False,
    )
```

profile of v0, /device:TPU:0, one launch (start us, length us, event | category | flops | bytes accessed | tf_op | source)
XLA Modules:
  0.0 37.0 jit_solution(16935307892668117895)
XLA Ops:
  0.0 2.1 %analyse.1 = f32[256,256]{1,0:T(8,128)} custom-call(f32[4,8,1024]{2,1,0:T(8,128)} %field_ref.1, bf16[256,384]{1,0:T(8,128)(2,1)} %constant.17.clone.table_ref), custom_call_target="tpu_custom_call" | custom-call | tf_op jit(solution)/shard_map/analyse/pallas_call | solution.py:209
  2.1 7.3 %all-to-all-start = ((f32[32,8,256]{2,1,0:T(8,128)}), f32[32,8,256]{2,1,0:T(8,128)S(1)}, u32[]{:S(2)}, u32[]{:S(2)}) async-start(f32[32,8,256]{2,1,0:T(8,128)} %bitcast.7), calls=%async_computation | async-start | bytes 524288 | tf_op jit(solution)/shard_map/all_to_all | solution.py:218
  9.5 0.1 fusion.11
  9.6 0.1 broadcast_add_fusion
  9.7 0.9 %fusion.4.spectrum_ref = f32[2,40,128]{2,1,0:T(8,128)} fusion(f32[]{:T(128)S(6)} %div.7, f32[128]{0:T(128)S(1)} %get-tuple-element.9, f32[40]{0:T(128)S(1)} %compare_select_fusion.1, f32[128]{0:T(128)S(1)} %get-tuple-element.10, f32[2,40]{1,0:T(2,128)S(1)} %broadcast_add_fusion), kind=kLoop, calls=%fused_computation.6 | loop fusion | flops 122880 | bytes 42468 | tf_op jit(solution)/shard_map/mul | solution.py:51
  10.5 3.8 %operator.1 = (bf16[2,2,2,256,256]{4,3,2,1,0:T(8,128)(2,1)}, bf16[2,2,2,256,256]{4,3,2,1,0:T(8,128)(2,1)}) custom-call(f32[2,40,128]{2,1,0:T(8,128)} %fusion.4.spectrum_ref, f32[128,1024]{1,0:T(8,128)} %constant.48.clone.cos_ref, f32[2,40,1024]{2,1,0:T(8,128)} %constant.49.clone.wave_ref, f32[2,16,40]{2,1,0:T(8,128)} %constant.50.clone.turn_ref), custom_call_target="tpu_custom_call" | custom-call | tf_op jit(solution)/shard_map/operator/pallas_call | solution.py:233
  14.3 5.7 %all-to-all-done.got_ref = f32[32,8,256]{2,1,0:T(8,128)S(1)} async-done(((f32[32,8,256]{2,1,0:T(8,128)}), f32[32,8,256]{2,1,0:T(8,128)S(1)}, u32[]{:S(2)}, u32[]{:S(2)}) %all-to-all-start) | async-done | bytes 262176 | tf_op jit(solution)/shard_map/all_to_all | solution.py:218
  20.0 0.0 copy-start
  20.0 0.7 %copy-done = f32[32,8,256]{2,1,0:T(8,128)} copy-done((f32[32,8,256]{2,1,0:T(8,128)}, f32[32,8,256]{2,1,0:T(8,128)S(1)}, u32[]{:S(2)}) %copy-start) | copy-done | bytes 262168
  20.8 3.3 %gram.1 = f32[32,128]{1,0:T(8,128)} custom-call(f32[32,8,256]{2,1,0:T(8,128)} %copy-done, bf16[2,2,2,256,256]{4,3,2,1,0:T(8,128)(2,1)} %get-tuple-element.7.high_ref, bf16[2,2,2,256,256]{4,3,2,1,0:T(8,128)(2,1)} %get-tuple-element.8.low_ref), custom_call_target="tpu_custom_call" | custom-call | tf_op jit(solution)/shard_map/gram/pallas_call | solution.py:246
  24.1 10.2 %all_to_all.16 = f32[32,1,128]{2,1,0:T(1,128)} all-to-all(f32[32,1,128]{2,1,0:T(1,128)} %bitcast.8), channel_id=1, replica_groups=mesh['vec'=8,'grid'=4] {'vec','grid'}, dimensions={0} | all-to-all | bytes 32768 | tf_op jit(solution)/shard_map/all_to_all | solution.py:253
  34.3 1.4 %finish.1 = f32[1,5,4]{2,1,0:T(8,128)} custom-call(f32[32,128]{1,0:T(8,128)} %bitcast.9), custom_call_target="tpu_custom_call" | custom-call | tf_op jit(solution)/shard_map/finish/pallas_call | solution.py:254
  35.7 1.3 %copy.8 = f32[1,5,4]{1,2,0:T(4,128)} copy(f32[1,5,4]{2,1,0:T(8,128)} %finish.1) | data formatting | bytes 160 | tf_op jit(solution)/shard_map/finish/pallas_call | solution.py:254
  (3 shorter events, 0.0 us)
Async XLA Ops:
  2.1 17.9 %all-to-all-start = ((f32[32,8,256]{2,1,0:T(8,128)}), f32[32,8,256]{2,1,0:T(8,128)S(1)}, u32[]{:S(2)}, u32[]{:S(2)}) async-start(f32[32,8,256]{2,1,0:T(8,128)} %bitcast.7), calls=%async_computation | async-start | bytes 524288 | tf_op jit(solution)/shard_map/all_to_all | solution.py:218
  20.0 0.7 %copy-start = (f32[32,8,256]{2,1,0:T(8,128)}, f32[32,8,256]{2,1,0:T(8,128)S(1)}, u32[]{:S(2)}) copy-start(f32[32,8,256]{2,1,0:T(8,128)S(1)} %all-to-all-done.got_ref) | copy-start | bytes 786436
where the time goes:
time: 37.4 us; the launch traced here: 37 us
  Pallas kernels  10.7 us (29%)
  blocking collectives  10.2 us (27%)
  starting transfers between devices  7.3 us (20%)
  waiting for transfers between devices  5.7 us (15%)
  local copies, waits for them, and re-layouts  2.05 us (5%)
  other arithmetic  1.03 us (3%)
    all_to_all x1, blocking collectives, tiled_program(): parts = lax.all_to_all(rows, AXES, 0, 0, tiled=True)  10.2 us
    all_to_all x1, starting transfers between devices, tiled_program(): got = lax.all_to_all(chunks, AXES, 0, 0, tiled=True)  7.3 us
    all_to_all x1, waiting for transfers between devices, tiled_program(): got = lax.all_to_all(chunks, AXES, 0, 0, tiled=True)  5.7 us
    pallas_call x1, Pallas kernels, tiled_program(): pl.pallas_call(functools.partial(operator_kernel, size), out_shape=(op_sh...  3.82 us
    pallas_call x1, Pallas kernels, tiled_program(): pl.pallas_call(functools.partial(gram_kernel, n_vec, n_grid, group), out_...  3.32 us
    pallas_call x1, Pallas kernels, tiled_program(): pl.pallas_call(functools.partial(analyse_kernel, size, n_grid), out_shape...  2.14 us
    pallas_call x1, Pallas kernels, tiled_program(): pl.pallas_call(finish_kernel, out_shape=jax.ShapeDtypeStruct((1, shifts,...  1.39 us
    pallas_call x1, local copies, waits for them, and re-layouts, tiled_program(): pl.pallas_call(finish_kernel, out_shape=jax.ShapeDtypeStruct((1, shifts,...  1.34 us
  transfers between devices with their start and end apart: 1, of which 1 were waited for; matrix products, arithmetic and copies ran while one was open for 3% of the time, Pallas kernels for 10%

commit v1 on v0

--- a/solution.py
+++ b/solution.py
@@ -12,6 +12,7 @@
 AXES = ("vec", "grid")
 LANES = 128
 ROWS = 8
+PARAMS = pltpu.CompilerParams(vmem_limit_bytes=16 * 2**20)
 
 
 def centred(size):
@@ -95,9 +96,10 @@
             rows.append(held_ref[parity, pl.ds(start, half, stride=slab), :])
         high, low = split_bf16(jnp.concatenate(rows, 0))
         operand = jnp.concatenate([high, high, low], 1)
-        out_ref[:, parity * LANES : (parity + 1) * LANES] = lax.dot_general(
+        values = lax.dot_general(
             table_ref[...], operand, (((1,), (1,)), ((), ())), preferred_element_type=jnp.float32
         )
+        out_ref[:, parity] = values.reshape(size, 2 * group, LANES)
 
 
 def operator_kernel(size, spectrum_ref, cos_ref, wave_ref, turn_ref, high_ref, low_ref):
@@ -134,33 +136,25 @@
 
 
 def gram_kernel(n_vec, n_grid, group, got_ref, high_ref, low_ref, out_ref):
-    per_tile = ROWS // group
     total = n_vec * group
-    row = lax.broadcasted_iota(jnp.int32, (ROWS, got_ref.shape[2]), 0)
+    tile = 2 * group
     left, right = [], []
     for c in range(2):
-        slabs = []
-        for i in range(n_grid):
-            tiles = []
-            for g in range(0, n_vec, 2):
-                first = got_ref[g * n_grid + i]
-                second = got_ref[(g + 1) * n_grid + i]
-                if c == 0:
-                    second = pltpu.roll(second, group, 0)
-                else:
-                    first = pltpu.roll(first, group, 0)
-                tiles.append(jnp.where(row < group, first, second))
-            slabs.append(jnp.concatenate(tiles, 0))
-        for sign in range(2):
-            folded = []
-            for i in range(n_grid // 2):
-                near, far = slabs[i], slabs[n_grid - 1 - i]
-                folded.append(near - far if sign else near + far)
-            for parity in range(2):
-                lanes = folded[0].shape[1] // 2
-                value = jnp.concatenate(
-                    [f[:, parity * lanes : (parity + 1) * lanes] for f in folded], 1
-                )
+        for parity in range(2):
+            slabs = []
+            for i in range(n_grid):
+                start = (i * 2 + parity) * tile + c * group
+                rows = [
+                    got_ref[pl.ds(start + v, n_vec, stride=n_grid * 2 * tile), :]
+                    for v in range(group)
+                ]
+                slabs.append(jnp.concatenate(rows, 0))
+            for sign in range(2):
+                folded = []
+                for i in range(n_grid // 2):
+                    near, far = slabs[i], slabs[n_grid - 1 - i]
+                    folded.append(near - far if sign else near + far)
+                value = jnp.concatenate(folded, 1)
                 high, low = split_bf16(value)
                 op_high, op_low = high_ref[c, parity, sign], low_ref[c, parity, sign]
                 both = jnp.dot(
@@ -171,25 +165,24 @@
                 applied_high, applied_low = split_bf16(applied)
                 left += [applied_high, applied_low, applied_high]
                 right += [high, high, low]
-    copies = LANES // total
     gram = lax.dot_general(
         jnp.concatenate(left, 1),
-        jnp.concatenate([jnp.concatenate(right, 1)] * copies, 0),
+        jnp.concatenate([jnp.concatenate(right, 1)] * (LANES // total), 0),
         (((1,), (1,)), ((), ())),
         preferred_element_type=jnp.float32,
     )
-    owner = lax.broadcasted_iota(jnp.int32, gram.shape, 0) // group
-    turned = gram
-    for g in range(1, n_vec):
-        turned = jnp.where(owner == g, pltpu.roll(gram, LANES - g * group, 1), turned)
-    out_ref[...] = turned
-
-
-def finish_kernel(got_ref, out_ref):
-    _, shifts, width = out_ref.shape
-    summed = jnp.sum(got_ref[...], 0, keepdims=True)
-    for s in range(shifts):
-        out_ref[0, s : s + 1, :] = summed[:, s * width : (s + 1) * width]
+    lane = lax.broadcasted_iota(jnp.int32, (n_vec, LANES), 1)
+    row = lax.broadcasted_iota(jnp.int32, (n_vec, LANES), 0)
+    for v in range(group):
+        held = gram[v * n_vec : (v + 1) * n_vec]
+        for w in range(group):
+            start = pltpu.roll(held, LANES - w * n_vec, 1) if w else held
+            wrapped = pltpu.roll(held, LANES - w * n_vec + n_vec, 1)
+            period = jnp.where(lane < n_vec, start, wrapped)
+            turned = period
+            for g in range(1, n_vec):
+                turned = jnp.where(row == g, pltpu.roll(period, LANES - g, 1), turned)
+            out_ref[pl.ds(v * group + w, n_vec, stride=group * group), :] = turned
 
 
 def whole_blocks(count):
@@ -208,14 +201,14 @@
     table = jnp.asarray(np.concatenate([high, low, high], 1))
     components = pl.pallas_call(
         functools.partial(analyse_kernel, size, n_grid),
-        out_shape=jax.ShapeDtypeStruct((size * 2 * group, size * slab), jnp.float32),
+        out_shape=jax.ShapeDtypeStruct((size, 2, 2 * group, LANES), jnp.float32),
         in_specs=whole_blocks(2),
         out_specs=whole_blocks(1)[0],
         scratch_shapes=[pltpu.VMEM((2, half * slab, LANES), jnp.float32)],
+        compiler_params=PARAMS,
         name="analyse",
     )(fitting_vectors, table)
-    chunks = components.reshape(n_devices, 2 * group, size * slab)
-    got = lax.all_to_all(chunks, AXES, 0, 0, tiled=True)
+    got = lax.all_to_all(components, AXES, 0, 0, tiled=True)
 
     omega = math.pi / size
     ky_pad = -(size + 1) % ROWS
@@ -235,6 +228,7 @@
         out_shape=(op_shape, op_shape),
         in_specs=whole_blocks(4),
         out_specs=tuple(whole_blocks(2)),
+        compiler_params=PARAMS,
         name="operator",
     )(
         spectrum,
@@ -245,19 +239,14 @@
 
     rows = pl.pallas_call(
         functools.partial(gram_kernel, n_vec, n_grid, group),
-        out_shape=jax.ShapeDtypeStruct((total, LANES), jnp.float32),
+        out_shape=jax.ShapeDtypeStruct((total * group, LANES), jnp.float32),
         in_specs=whole_blocks(3),
         out_specs=whole_blocks(1)[0],
+        compiler_params=PARAMS,
         name="gram",
-    )(got, op_high, op_low)
-    parts = lax.all_to_all(rows, AXES, 0, 0, tiled=True)
-    return pl.pallas_call(
-        finish_kernel,
-        out_shape=jax.ShapeDtypeStruct((1, shifts, group), jnp.float32),
-        in_specs=whole_blocks(1),
-        out_specs=whole_blocks(1)[0],
-        name="finish",
-    )(parts)
+    )(got.reshape(n_devices * 4 * group, LANES), op_high, op_low)
+    parts = lax.all_to_all(rows.reshape(total, group, LANES), AXES, 0, 0, tiled=True)
+    return jnp.sum(parts[:, :, :shifts], 0).T[None]
 
 
 def general_program(fitting_vectors, size, n_vec, n_grid, shifts):

time: 37.4 us -> 32.8 us (0.88)
  Pallas kernels: 10.7 us -> 3.78 us
  waiting for transfers between devices: 5.7 us -> 8.32 us
  blocking collectives: 10.2 us -> 9.62 us
    all_to_all x1, waiting for transfers between devices: 5.7 us -> 8.32 us  [tiled_program(): got = lax.all_to_all(components, AXES, 0, 0, tiled=True)]
    pallas_call x1, Pallas kernels: 3.82 us -> 1.35 us  [tiled_program(): pl.pallas_call(functools.partial(operator_kernel, size), out_shape=(op_sh...]
    pallas_call x1, Pallas kernels: 3.32 us -> 1.29 us  [tiled_program(): pl.pallas_call(functools.partial(gram_kernel, n_vec, n_grid, group), out_...]
    unnamed x2 -> x10, local copies, waits for them, and re-layouts: 0.71 us -> 2.34 us
    pallas_call x1 -> x0, Pallas kernels: 1.39 us -> none  [tiled_program(): pl.pallas_call(finish_kernel, out_shape=jax.ShapeDtypeStruct((1, shifts,...]
    pallas_call x1 -> x0, local copies, waits for them, and re-layouts: 1.34 us -> none  [tiled_program(): pl.pallas_call(finish_kernel, out_shape=jax.ShapeDtypeStruct((1, shifts,...]
    pallas_call x1, Pallas kernels: 2.14 us -> 1.15 us  [tiled_program(): pl.pallas_call(functools.partial(analyse_kernel, size, n_grid), out_shape...]
    mul x1, other arithmetic: 0.87 us -> 0.25 us  [operator_spectrum(): values * weight(ky)[None, :, None] * weight(kx)[None, None, :] * scale]
  transfers between devices with their start and end apart: 1 -> 1, of which waited for: 1 -> 1; matrix products, arithmetic and copies ran while one was open for 3% -> 1% of each run, Pallas kernels for 10% -> 4%
where the time goes in v1:
time: 32.8 us; the launch traced here: 32.5 us
  blocking collectives  9.62 us (29%)
  waiting for transfers between devices  8.32 us (25%)
  starting transfers between devices  7.29 us (22%)
  Pallas kernels  3.78 us (12%)
  local copies, waits for them, and re-layouts  2.34 us (7%)
  other arithmetic  1.03 us (3%)
    all_to_all x1, blocking collectives, tiled_program(): lax.all_to_all(rows.reshape(total, group, LANES), AXES, 0, 0, tiled=True)  9.62 us
    all_to_all x1, waiting for transfers between devices, tiled_program(): got = lax.all_to_all(components, AXES, 0, 0, tiled=True)  8.32 us
    all_to_all x1, starting transfers between devices, tiled_program(): got = lax.all_to_all(components, AXES, 0, 0, tiled=True)  7.29 us
    unnamed x10, local copies, waits for them, and re-layouts  2.34 us
    pallas_call x1, Pallas kernels, tiled_program(): pl.pallas_call(functools.partial(operator_kernel, size), out_shape=(op_sh...  1.35 us
    pallas_call x1, Pallas kernels, tiled_program(): pl.pallas_call(functools.partial(gram_kernel, n_vec, n_grid, group), out_...  1.29 us
    pallas_call x1, Pallas kernels, tiled_program(): pl.pallas_call(functools.partial(analyse_kernel, size, n_grid), out_shape...  1.15 us
  transfers between devices with their start and end apart: 1, of which 1 were waited for; matrix products, arithmetic and copies ran while one was open for 1% of the time, Pallas kernels for 4%

profile of v1, /device:TPU:0, one launch (start us, length us, event | category | flops | bytes accessed | tf_op | source)
XLA Modules:
  0.0 32.5 jit_solution(18436193160314021741)
XLA Ops:
  0.0 0.0 copy-start
  0.0 0.0 copy-start.2
  0.0 1.0 %copy-done.2 = bf16[256,384]{1,0:T(8,128)(2,1)S(1)} copy-done((bf16[256,384]{1,0:T(8,128)(2,1)S(1)}, bf16[256,384]{1,0:T(8,128)(2,1)}, u32[]{:S(2)}) %copy-start.2) | copy-done | bytes 196632
  1.0 0.0 copy-start.3
  1.0 0.9 %copy-done.3 = f32[4,8,1024]{2,1,0:T(8,128)S(1)} copy-done((f32[4,8,1024]{2,1,0:T(8,128)S(1)}, f32[4,8,1024]{2,1,0:T(8,128)}, u32[]{:S(2)}) %copy-start.3) | copy-done | bytes 131096
  1.9 1.1 %analyse.1 = f32[32,2,8,128]{3,2,1,0:T(8,128)} custom-call(f32[4,8,1024]{2,1,0:T(8,128)S(1)} %copy-done.3, bf16[256,384]{1,0:T(8,128)(2,1)S(1)} %copy-done.2), custom_call_target="tpu_custom_call" | custom-call | tf_op jit(solution)/shard_map/analyse/pallas_call | solution.py:202
  3.0 0.0 copy-start.1
  3.0 7.3 %all-to-all-start = ((f32[32,2,8,128]{3,2,1,0:T(8,128)}), f32[32,2,8,128]{3,2,1,0:T(8,128)S(1)}, u32[]{:S(2)}, u32[]{:S(2)}) async-start(f32[32,2,8,128]{3,2,1,0:T(8,128)} %analyse.1), calls=%async_computation | async-start | bytes 524288 | tf_op jit(solution)/shard_map/all_to_all | solution.py:211
  10.4 0.1 fusion.11
  10.5 0.1 broadcast_add_fusion
  10.5 0.0 copy-start.4
  10.6 0.2 fusion.4.spectrum_ref
  10.8 0.0 copy-done
  10.8 0.0 copy-done.1
  10.8 0.4 %copy-done.4 = f32[2,16,40]{2,1,0:T(8,128)S(1)} copy-done((f32[2,16,40]{2,1,0:T(8,128)S(1)}, f32[2,16,40]{2,1,0:T(8,128)}, u32[]{:S(2)}) %copy-start.4) | copy-done | bytes 5144
  11.3 1.3 %operator.1 = (bf16[2,2,2,256,256]{4,3,2,1,0:T(8,128)(2,1)S(1)}, bf16[2,2,2,256,256]{4,3,2,1,0:T(8,128)(2,1)S(1)}) custom-call(f32[2,40,128]{2,1,0:T(8,128)S(1)} %fusion.4.spectrum_ref, f32[128,1024]{1,0:T(8,128)S(1)} %copy-done, f32[2,40,1024]{2,1,0:T(8,128)S(1)} %copy-done.1, f32[2,16,40]{2,1,0:T(8,128)S(1)} %copy-done.4), custom_call_target="tpu_custom_call" | custom-call | tf_op jit(solution)/shard_map/operator/pallas_call | solution.py:226
  12.6 8.3 %all-to-all-done = f32[32,2,8,128]{3,2,1,0:T(8,128)S(1)} async-done(((f32[32,2,8,128]{3,2,1,0:T(8,128)}), f32[32,2,8,128]{3,2,1,0:T(8,128)S(1)}, u32[]{:S(2)}, u32[]{:S(2)}) %all-to-all-start) | async-done | bytes 262176 | tf_op jit(solution)/shard_map/all_to_all | solution.py:211
  20.9 1.3 %gram.1 = f32[128,128]{1,0:T(8,128)S(1)} custom-call(f32[512,128]{1,0:T(8,128)S(1)} %bitcast.7, bf16[2,2,2,256,256]{4,3,2,1,0:T(8,128)(2,1)S(1)} %get-tuple-element.7.high_ref, bf16[2,2,2,256,256]{4,3,2,1,0:T(8,128)(2,1)S(1)} %get-tuple-element.8.low_ref), custom_call_target="tpu_custom_call" | custom-call | tf_op jit(solution)/shard_map/gram/pallas_call | solution.py:240
  22.2 9.6 %all_to_all.10 = f32[32,4,128]{2,1,0:T(4,128)S(1)} all-to-all(f32[32,4,128]{2,1,0:T(4,128)S(1)} %bitcast.8), channel_id=1, replica_groups=mesh['vec'=8,'grid'=4] {'vec','grid'}, dimensions={0} | all-to-all | bytes 131072 | tf_op jit(solution)/shard_map/all_to_all | solution.py:248
  31.9 0.6 %slice_reduce_fusion = f32[4,5]{1,0:T(4,128)} fusion(f32[32,4,128]{2,1,0:T(4,128)S(1)} %all_to_all.10), kind=kLoop, calls=%fused_computation | loop fusion | flops 620 | bytes 2640 | tf_op jit(solution)/shard_map/reduce_sum | solution.py:249
  (3 shorter events, 0.0 us)
Async XLA Ops:
  0.0 10.8 %copy-start = (f32[128,1024]{1,0:T(8,128)S(1)}, f32[128,1024]{1,0:T(8,128)}, u32[]{:S(2)}) copy-start(f32[128,1024]{1,0:T(8,128)} %constant.48.clone.cos_ref) | copy-start | bytes 1572868
  0.0 1.0 %copy-start.2 = (bf16[256,384]{1,0:T(8,128)(2,1)S(1)}, bf16[256,384]{1,0:T(8,128)(2,1)}, u32[]{:S(2)}) copy-start(bf16[256,384]{1,0:T(8,128)(2,1)} %constant.17.clone.table_ref) | copy-start | bytes 589828
  1.0 0.9 %copy-start.3 = (f32[4,8,1024]{2,1,0:T(8,128)S(1)}, f32[4,8,1024]{2,1,0:T(8,128)}, u32[]{:S(2)}) copy-start(f32[4,8,1024]{2,1,0:T(8,128)} %field_ref.1) | copy-start | bytes 393220
  3.0 7.8 %copy-start.1 = (f32[2,40,1024]{2,1,0:T(8,128)S(1)}, f32[2,40,1024]{2,1,0:T(8,128)}, u32[]{:S(2)}) copy-start(f32[2,40,1024]{2,1,0:T(8,128)} %constant.49.clone.wave_ref) | copy-start | bytes 983044
  3.0 17.9 %all-to-all-start = ((f32[32,2,8,128]{3,2,1,0:T(8,128)}), f32[32,2,8,128]{3,2,1,0:T(8,128)S(1)}, u32[]{:S(2)}, u32[]{:S(2)}) async-start(f32[32,2,8,128]{3,2,1,0:T(8,128)} %analyse.1), calls=%async_computation | async-start | bytes 524288 | tf_op jit(solution)/shard_map/all_to_all | solution.py:211
  10.5 0.7 %copy-start.4 = (f32[2,16,40]{2,1,0:T(8,128)S(1)}, f32[2,16,40]{2,1,0:T(8,128)}, u32[]{:S(2)}) copy-start(f32[2,16,40]{2,1,0:T(8,128)} %constant.50.clone.turn_ref) | copy-start | bytes 15364

commit v2 on v1

--- a/solution.py
+++ b/solution.py
@@ -13,6 +13,7 @@
 LANES = 128
 ROWS = 8
 PARAMS = pltpu.CompilerParams(vmem_limit_bytes=16 * 2**20)
+ALL_VMEM = pltpu.CompilerParams(vmem_limit_bytes=60 * 2**20)
 
 
 def centred(size):
@@ -63,12 +64,20 @@
     return high, (table - high.astype(np.float32)).astype(jnp.bfloat16)
 
 
-def analyse_kernel(size, n_grid, field_ref, table_ref, out_ref, held_ref):
+def analyse_kernel(
+    size, n_grid, field_hbm, table_hbm, out_hbm, field_ref, table_ref, held_ref, out_ref, sems
+):
     group, slab, _ = field_ref.shape
     half = size // 2
     per_block = LANES // size
     blocks = size // per_block
+    field_copy = pltpu.make_async_copy(field_hbm, field_ref, sems.at[0])
+    table_copy = pltpu.make_async_copy(table_hbm, table_ref, sems.at[1])
+    field_copy.start()
+    table_copy.start()
+    mirrored = lax.axis_index("grid") >= n_grid // 2
     lane_group = lax.broadcasted_iota(jnp.int32, (blocks * slab, LANES), 1) // size
+    field_copy.wait()
     stacked = [
         jnp.concatenate([field_ref[v, :, b * LANES : (b + 1) * LANES] for b in range(blocks)], 0)
         for v in range(group)
@@ -88,18 +97,24 @@
         far = turned[other_q][other_b * slab : (other_b + 1) * slab]
         held_ref[0, y * slab : (y + 1) * slab, :] = near + far
         held_ref[1, y * slab : (y + 1) * slab, :] = near - far
-    mirrored = lax.axis_index("grid") >= n_grid // 2
+    rows = []
     for parity in range(2):
-        rows = []
         for j in range(slab):
             start = jnp.where(mirrored, slab - 1 - j, j)
             rows.append(held_ref[parity, pl.ds(start, half, stride=slab), :])
-        high, low = split_bf16(jnp.concatenate(rows, 0))
-        operand = jnp.concatenate([high, high, low], 1)
-        values = lax.dot_general(
-            table_ref[...], operand, (((1,), (1,)), ((), ())), preferred_element_type=jnp.float32
-        )
-        out_ref[:, parity] = values.reshape(size, 2 * group, LANES)
+    high, low = split_bf16(jnp.concatenate(rows, 0))
+    operand = jnp.concatenate([high, high, low], 1)
+    table_copy.wait()
+    table = jnp.concatenate([table_ref[...], table_ref[:, :LANES]], 1)
+    values = lax.dot_general(
+        table, operand, (((1,), (1,)), ((), ())), preferred_element_type=jnp.float32
+    )
+    for parity in range(2):
+        part = values[:, parity * LANES : (parity + 1) * LANES]
+        out_ref[:, parity] = part.reshape(size, 2 * group, LANES)
+    out_copy = pltpu.make_async_copy(out_ref, out_hbm, sems.at[2])
+    out_copy.start()
+    out_copy.wait()
 
 
 def operator_kernel(size, spectrum_ref, cos_ref, wave_ref, turn_ref, high_ref, low_ref):
@@ -162,15 +177,17 @@
                 )
                 applied = both[:total] + both[total:]
                 applied += jnp.dot(high, op_low, preferred_element_type=jnp.float32)
-                applied_high, applied_low = split_bf16(applied)
-                left += [applied_high, applied_low, applied_high]
-                right += [high, high, low]
+                left.append(jnp.concatenate(split_bf16(applied), 0))
+                right.append(jnp.concatenate([high, low], 0))
     gram = lax.dot_general(
         jnp.concatenate(left, 1),
-        jnp.concatenate([jnp.concatenate(right, 1)] * (LANES // total), 0),
+        jnp.concatenate(right, 1),
         (((1,), (1,)), ((), ())),
         preferred_element_type=jnp.float32,
     )
+    gram = gram[:total] + gram[total:]
+    gram = gram[:, :total] + gram[:, total:]
+    gram = jnp.concatenate([gram, jnp.zeros((total, LANES - total), jnp.float32)], 1)
     lane = lax.broadcasted_iota(jnp.int32, (n_vec, LANES), 1)
     row = lax.broadcasted_iota(jnp.int32, (n_vec, LANES), 0)
     for v in range(group):
@@ -198,14 +215,21 @@
 
     spread = np.einsum("kcz,vw->kcvwz", pair_table(size), np.eye(group))
     high, low = split_table(spread.reshape(size * 2 * group, group * size))
-    table = jnp.asarray(np.concatenate([high, low, high], 1))
+    table = jnp.asarray(np.concatenate([high, low], 1))
+    chunk_shape = (size, 2, 2 * group, LANES)
     components = pl.pallas_call(
         functools.partial(analyse_kernel, size, n_grid),
-        out_shape=jax.ShapeDtypeStruct((size, 2, 2 * group, LANES), jnp.float32),
-        in_specs=whole_blocks(2),
-        out_specs=whole_blocks(1)[0],
-        scratch_shapes=[pltpu.VMEM((2, half * slab, LANES), jnp.float32)],
-        compiler_params=PARAMS,
+        out_shape=jax.ShapeDtypeStruct(chunk_shape, jnp.float32),
+        in_specs=[pl.BlockSpec(memory_space=pltpu.HBM)] * 2,
+        out_specs=pl.BlockSpec(memory_space=pltpu.HBM),
+        scratch_shapes=[
+            pltpu.VMEM(fitting_vectors.shape, jnp.float32),
+            pltpu.VMEM(table.shape, table.dtype),
+            pltpu.VMEM((2, half * slab, LANES), jnp.float32),
+            pltpu.VMEM(chunk_shape, jnp.float32),
+            pltpu.SemaphoreType.DMA((3,)),
+        ],
+        compiler_params=ALL_VMEM,
         name="analyse",
     )(fitting_vectors, table)
     got = lax.all_to_all(components, AXES, 0, 0, tiled=True)

time: 32.8 us -> 31.7 us (0.966)
  local copies, waits for them, and re-layouts: 2.34 us -> 0.46 us
  Pallas kernels: 3.78 us -> 4.5 us
    unnamed x10 -> x6, local copies, waits for them, and re-layouts: 2.34 us -> 0.46 us
    pallas_call x1, Pallas kernels: 1.15 us -> 2.15 us  [tiled_program(): pl.pallas_call(functools.partial(analyse_kernel, size, n_grid), out_shape...]
where the time goes in v2:
time: 31.7 us; the launch traced here: 31.3 us
  blocking collectives  9.62 us (30%)
  waiting for transfers between devices  8.32 us (26%)
  starting transfers between devices  7.31 us (23%)
  Pallas kernels  4.5 us (14%)
  other arithmetic  1.03 us (3%)
  local copies, waits for them, and re-layouts  0.46 us (1%)
    all_to_all x1, blocking collectives, tiled_program(): lax.all_to_all(rows.reshape(total, group, LANES), AXES, 0, 0, tiled=True)  9.62 us
    all_to_all x1, waiting for transfers between devices, tiled_program(): got = lax.all_to_all(components, AXES, 0, 0, tiled=True)  8.32 us
    all_to_all x1, starting transfers between devices, tiled_program(): got = lax.all_to_all(components, AXES, 0, 0, tiled=True)  7.31 us
    pallas_call x1, Pallas kernels, tiled_program(): pl.pallas_call(functools.partial(analyse_kernel, size, n_grid), out_shape...  2.15 us
    pallas_call x1, Pallas kernels, tiled_program(): pl.pallas_call(functools.partial(operator_kernel, size), out_shape=(op_sh...  1.34 us
    pallas_call x1, Pallas kernels, tiled_program(): pl.pallas_call(functools.partial(gram_kernel, n_vec, n_grid, group), out_...  1.01 us
  transfers between devices with their start and end apart: 1, of which 1 were waited for; matrix products, arithmetic and copies ran while one was open for 1% of the time, Pallas kernels for 4%

profile of v2, /device:TPU:0, one launch (start us, length us, event | category | flops | bytes accessed | tf_op | source)
XLA Modules:
  0.0 31.3 jit_solution(13421793715034940092)
XLA Ops:
  0.0 0.0 copy-start
  0.0 2.1 %analyse.1 = f32[32,2,8,128]{3,2,1,0:T(8,128)} custom-call(f32[4,8,1024]{2,1,0:T(8,128)} %field_hbm.1, bf16[256,256]{1,0:T(8,128)(2,1)} %constant.17.clone.table_hbm), custom_call_target="tpu_custom_call" | custom-call | tf_op jit(solution)/shard_map/analyse/pallas_call | solution.py:220
  2.2 0.0 copy-start.1
  2.2 7.3 %all-to-all-start = ((f32[32,2,8,128]{3,2,1,0:T(8,128)}), f32[32,2,8,128]{3,2,1,0:T(8,128)S(1)}, u32[]{:S(2)}, u32[]{:S(2)}) async-start(f32[32,2,8,128]{3,2,1,0:T(8,128)} %analyse.1), calls=%async_computation | async-start | bytes 524288 | tf_op jit(solution)/shard_map/all_to_all | solution.py:235
  9.5 0.1 fusion.11
  9.6 0.1 broadcast_add_fusion
  9.7 0.0 copy-start.2
  9.7 0.2 fusion.4.spectrum_ref
  9.9 0.0 copy-done
  10.0 0.0 copy-done.1
  10.0 0.4 %copy-done.2 = f32[2,16,40]{2,1,0:T(8,128)S(1)} copy-done((f32[2,16,40]{2,1,0:T(8,128)S(1)}, f32[2,16,40]{2,1,0:T(8,128)}, u32[]{:S(2)}) %copy-start.2) | copy-done | bytes 5144
  10.4 1.3 %operator.1 = (bf16[2,2,2,256,256]{4,3,2,1,0:T(8,128)(2,1)S(1)}, bf16[2,2,2,256,256]{4,3,2,1,0:T(8,128)(2,1)S(1)}) custom-call(f32[2,40,128]{2,1,0:T(8,128)S(1)} %fusion.4.spectrum_ref, f32[128,1024]{1,0:T(8,128)S(1)} %copy-done, f32[2,40,1024]{2,1,0:T(8,128)S(1)} %copy-done.1, f32[2,16,40]{2,1,0:T(8,128)S(1)} %copy-done.2), custom_call_target="tpu_custom_call" | custom-call | tf_op jit(solution)/shard_map/operator/pallas_call | solution.py:250
  11.8 8.3 %all-to-all-done = f32[32,2,8,128]{3,2,1,0:T(8,128)S(1)} async-done(((f32[32,2,8,128]{3,2,1,0:T(8,128)}), f32[32,2,8,128]{3,2,1,0:T(8,128)S(1)}, u32[]{:S(2)}, u32[]{:S(2)}) %all-to-all-start) | async-done | bytes 262176 | tf_op jit(solution)/shard_map/all_to_all | solution.py:235
  20.1 1.0 %gram.1 = f32[128,128]{1,0:T(8,128)S(1)} custom-call(f32[512,128]{1,0:T(8,128)S(1)} %bitcast.7, bf16[2,2,2,256,256]{4,3,2,1,0:T(8,128)(2,1)S(1)} %get-tuple-element.7.high_ref, bf16[2,2,2,256,256]{4,3,2,1,0:T(8,128)(2,1)S(1)} %get-tuple-element.8.low_ref), custom_call_target="tpu_custom_call" | custom-call | tf_op jit(solution)/shard_map/gram/pallas_call | solution.py:264
  21.1 9.6 %all_to_all.10 = f32[32,4,128]{2,1,0:T(4,128)S(1)} all-to-all(f32[32,4,128]{2,1,0:T(4,128)S(1)} %bitcast.8), channel_id=1, replica_groups=mesh['vec'=8,'grid'=4] {'vec','grid'}, dimensions={0} | all-to-all | bytes 131072 | tf_op jit(solution)/shard_map/all_to_all | solution.py:272
  30.7 0.6 %slice_reduce_fusion = f32[4,5]{1,0:T(4,128)} fusion(f32[32,4,128]{2,1,0:T(4,128)S(1)} %all_to_all.10), kind=kLoop, calls=%fused_computation | loop fusion | flops 620 | bytes 2640 | tf_op jit(solution)/shard_map/reduce_sum | solution.py:273
  (3 shorter events, 0.0 us)
Async XLA Ops:
  0.0 9.9 %copy-start = (f32[128,1024]{1,0:T(8,128)S(1)}, f32[128,1024]{1,0:T(8,128)}, u32[]{:S(2)}) copy-start(f32[128,1024]{1,0:T(8,128)} %constant.48.clone.cos_ref) | copy-start | bytes 1572868
  2.2 7.8 %copy-start.1 = (f32[2,40,1024]{2,1,0:T(8,128)S(1)}, f32[2,40,1024]{2,1,0:T(8,128)}, u32[]{:S(2)}) copy-start(f32[2,40,1024]{2,1,0:T(8,128)} %constant.49.clone.wave_ref) | copy-start | bytes 983044
  2.2 17.9 %all-to-all-start = ((f32[32,2,8,128]{3,2,1,0:T(8,128)}), f32[32,2,8,128]{3,2,1,0:T(8,128)S(1)}, u32[]{:S(2)}, u32[]{:S(2)}) async-start(f32[32,2,8,128]{3,2,1,0:T(8,128)} %analyse.1), calls=%async_computation | async-start | bytes 524288 | tf_op jit(solution)/shard_map/all_to_all | solution.py:235
  9.7 0.7 %copy-start.2 = (f32[2,16,40]{2,1,0:T(8,128)S(1)}, f32[2,16,40]{2,1,0:T(8,128)}, u32[]{:S(2)}) copy-start(f32[2,16,40]{2,1,0:T(8,128)} %constant.50.clone.turn_ref) | copy-start | bytes 15364

commit v3 on v2

--- a/solution.py
+++ b/solution.py
@@ -153,6 +153,7 @@
 def gram_kernel(n_vec, n_grid, group, got_ref, high_ref, low_ref, out_ref):
     total = n_vec * group
     tile = 2 * group
+
     left, right = [], []
     for c in range(2):
         for parity in range(2):
@@ -186,20 +187,23 @@
         preferred_element_type=jnp.float32,
     )
     gram = gram[:total] + gram[total:]
-    gram = gram[:, :total] + gram[:, total:]
-    gram = jnp.concatenate([gram, jnp.zeros((total, LANES - total), jnp.float32)], 1)
-    lane = lax.broadcasted_iota(jnp.int32, (n_vec, LANES), 1)
-    row = lax.broadcasted_iota(jnp.int32, (n_vec, LANES), 0)
-    for v in range(group):
-        held = gram[v * n_vec : (v + 1) * n_vec]
-        for w in range(group):
-            start = pltpu.roll(held, LANES - w * n_vec, 1) if w else held
-            wrapped = pltpu.roll(held, LANES - w * n_vec + n_vec, 1)
-            period = jnp.where(lane < n_vec, start, wrapped)
-            turned = period
-            for g in range(1, n_vec):
-                turned = jnp.where(row == g, pltpu.roll(period, LANES - g, 1), turned)
-            out_ref[pl.ds(v * group + w, n_vec, stride=group * group), :] = turned
+    gram = jnp.concatenate([gram, jnp.zeros((total, LANES - 2 * total), jnp.float32)], 1)
+    gram += pltpu.roll(gram, LANES - total, 1)
+    owner = lax.broadcasted_iota(jnp.int32, gram.shape, 0) % n_vec
+    place = lax.broadcasted_iota(jnp.int32, gram.shape, 1) % n_vec
+    step = 1
+    while step < n_vec:
+        ahead = pltpu.roll(gram, LANES - step, 1)
+        behind = pltpu.roll(gram, n_vec - step, 1)
+        turned = jnp.where(place < n_vec - step, ahead, behind)
+        gram = jnp.where(owner // step % 2 == 1, turned, gram)
+        step *= 2
+    for w in range(group):
+        turned = pltpu.roll(gram, LANES - w * n_vec, 1) if w else gram
+        for v in range(group):
+            out_ref[pl.ds(v * group + w, n_vec, stride=group * group), :] = turned[
+                v * n_vec : (v + 1) * n_vec
+            ]
 
 
 def whole_blocks(count):
@@ -236,7 +240,7 @@
 
     omega = math.pi / size
     ky_pad = -(size + 1) % ROWS
-    kx_pad = -(size + 1) % LANES
+    kx_pad = -(size + 1) % ROWS
     spectrum = operator_spectrum(size, pair, kx_pad, ky_pad)
     freqs_y = np.arange(size + 1 + ky_pad)
     freqs_x = np.arange(size + 1 + kx_pad)

time: 31.7 us -> 31.6 us (level)
  no operation moved by 1% of the time
where the time goes in v3:
time: 31.6 us; the launch traced here: 31.3 us
  blocking collectives  9.62 us (30%)
  waiting for transfers between devices  8.46 us (27%)
  starting transfers between devices  7.3 us (23%)
  Pallas kernels  4.36 us (14%)
  other arithmetic  1.02 us (3%)
  local copies, waits for them, and re-layouts  0.46 us (1%)
    all_to_all x1, blocking collectives, tiled_program(): lax.all_to_all(rows.reshape(total, group, LANES), AXES, 0, 0, tiled=True)  9.62 us
    all_to_all x1, waiting for transfers between devices, tiled_program(): got = lax.all_to_all(components, AXES, 0, 0, tiled=True)  8.46 us
    all_to_all x1, starting transfers between devices, tiled_program(): got = lax.all_to_all(components, AXES, 0, 0, tiled=True)  7.3 us
    pallas_call x1, Pallas kernels, tiled_program(): pl.pallas_call(functools.partial(analyse_kernel, size, n_grid), out_shape...  2.1 us
    pallas_call x1, Pallas kernels, tiled_program(): pl.pallas_call(functools.partial(operator_kernel, size), out_shape=(op_sh...  1.23 us
    pallas_call x1, Pallas kernels, tiled_program(): pl.pallas_call(functools.partial(gram_kernel, n_vec, n_grid, group), out_...  1.03 us
  transfers between devices with their start and end apart: 1, of which 1 were waited for; matrix products, arithmetic and copies ran while one was open for 1% of the time, Pallas kernels for 4%

profile of v3, /device:TPU:0, one launch (start us, length us, event | category | flops | bytes accessed | tf_op | source)
XLA Modules:
  0.0 31.3 jit_solution(16086747854890693989)
XLA Ops:
  0.0 2.1 %analyse.1 = f32[32,2,8,128]{3,2,1,0:T(8,128)} custom-call(f32[4,8,1024]{2,1,0:T(8,128)} %field_hbm.1, bf16[256,256]{1,0:T(8,128)(2,1)} %constant.45.clone.table_hbm), custom_call_target="tpu_custom_call" | custom-call | tf_op jit(solution)/shard_map/analyse/pallas_call | solution.py:224
  2.1 0.0 copy-start
  2.1 0.0 copy-start.1
  2.1 7.3 %all-to-all-start = ((f32[32,2,8,128]{3,2,1,0:T(8,128)}), f32[32,2,8,128]{3,2,1,0:T(8,128)S(1)}, u32[]{:S(2)}, u32[]{:S(2)}) async-start(f32[32,2,8,128]{3,2,1,0:T(8,128)} %analyse.1), calls=%async_computation | async-start | bytes 524288 | tf_op jit(solution)/shard_map/all_to_all | solution.py:239
  9.5 0.1 fusion.11
  9.5 0.1 broadcast_add_fusion
  9.6 0.0 copy-start.2
  9.6 0.2 fusion.4.spectrum_ref
  9.9 0.0 copy-done
  9.9 0.0 copy-done.1
  9.9 0.4 %copy-done.2 = f32[2,16,40]{2,1,0:T(8,128)S(1)} copy-done((f32[2,16,40]{2,1,0:T(8,128)S(1)}, f32[2,16,40]{2,1,0:T(8,128)}, u32[]{:S(2)}) %copy-start.2) | copy-done | bytes 5144
  10.3 1.2 %operator.1 = (bf16[2,2,2,256,256]{4,3,2,1,0:T(8,128)(2,1)S(1)}, bf16[2,2,2,256,256]{4,3,2,1,0:T(8,128)(2,1)S(1)}) custom-call(f32[2,40,40]{2,1,0:T(8,128)S(1)} %fusion.4.spectrum_ref, f32[40,1024]{1,0:T(8,128)S(1)} %copy-done.1, f32[2,40,1024]{2,1,0:T(8,128)S(1)} %copy-done, f32[2,16,40]{2,1,0:T(8,128)S(1)} %copy-done.2), custom_call_target="tpu_custom_call" | custom-call | tf_op jit(solution)/shard_map/operator/pallas_call | solution.py:254
  11.6 8.5 %all-to-all-done = f32[32,2,8,128]{3,2,1,0:T(8,128)S(1)} async-done(((f32[32,2,8,128]{3,2,1,0:T(8,128)}), f32[32,2,8,128]{3,2,1,0:T(8,128)S(1)}, u32[]{:S(2)}, u32[]{:S(2)}) %all-to-all-start) | async-done | bytes 262176 | tf_op jit(solution)/shard_map/all_to_all | solution.py:239
  20.0 1.0 %gram.1 = f32[128,128]{1,0:T(8,128)S(1)} custom-call(f32[512,128]{1,0:T(8,128)S(1)} %bitcast.7, bf16[2,2,2,256,256]{4,3,2,1,0:T(8,128)(2,1)S(1)} %get-tuple-element.7.high_ref, bf16[2,2,2,256,256]{4,3,2,1,0:T(8,128)(2,1)S(1)} %get-tuple-element.8.low_ref), custom_call_target="tpu_custom_call" | custom-call | tf_op jit(solution)/shard_map/gram/pallas_call | solution.py:268
  21.1 9.6 %all_to_all.10 = f32[32,4,128]{2,1,0:T(4,128)S(1)} all-to-all(f32[32,4,128]{2,1,0:T(4,128)S(1)} %bitcast.8), channel_id=1, replica_groups=mesh['vec'=8,'grid'=4] {'vec','grid'}, dimensions={0} | all-to-all | bytes 131072 | tf_op jit(solution)/shard_map/all_to_all | solution.py:276
  30.7 0.6 %slice_reduce_fusion = f32[4,5]{1,0:T(4,128)} fusion(f32[32,4,128]{2,1,0:T(4,128)S(1)} %all_to_all.10), kind=kLoop, calls=%fused_computation | loop fusion | flops 620 | bytes 2640 | tf_op jit(solution)/shard_map/reduce_sum | solution.py:277
  (1 shorter events, 0.0 us)
Async XLA Ops:
  2.1 7.8 %copy-start = (f32[2,40,1024]{2,1,0:T(8,128)S(1)}, f32[2,40,1024]{2,1,0:T(8,128)}, u32[]{:S(2)}) copy-start(f32[2,40,1024]{2,1,0:T(8,128)} %constant.47.clone.wave_ref) | copy-start | bytes 983044
  2.1 7.8 %copy-start.1 = (f32[40,1024]{1,0:T(8,128)S(1)}, f32[40,1024]{1,0:T(8,128)}, u32[]{:S(2)}) copy-start(f32[40,1024]{1,0:T(8,128)} %constant.46.clone.cos_ref) | copy-start | bytes 491524
  2.1 17.9 %all-to-all-start = ((f32[32,2,8,128]{3,2,1,0:T(8,128)}), f32[32,2,8,128]{3,2,1,0:T(8,128)S(1)}, u32[]{:S(2)}, u32[]{:S(2)}) async-start(f32[32,2,8,128]{3,2,1,0:T(8,128)} %analyse.1), calls=%async_computation | async-start | bytes 524288 | tf_op jit(solution)/shard_map/all_to_all | solution.py:239
  9.6 0.7 %copy-start.2 = (f32[2,16,40]{2,1,0:T(8,128)S(1)}, f32[2,16,40]{2,1,0:T(8,128)}, u32[]{:S(2)}) copy-start(f32[2,16,40]{2,1,0:T(8,128)} %constant.48.clone.turn_ref) | copy-start | bytes 15364

commit v4 on v3

--- a/solution.py
+++ b/solution.py
@@ -12,6 +12,7 @@
 AXES = ("vec", "grid")
 LANES = 128
 ROWS = 8
+OUT_COPIES = 4
 PARAMS = pltpu.CompilerParams(vmem_limit_bytes=16 * 2**20)
 ALL_VMEM = pltpu.CompilerParams(vmem_limit_bytes=60 * 2**20)
 
@@ -71,13 +72,17 @@
     half = size // 2
     per_block = LANES // size
     blocks = size // per_block
-    field_copy = pltpu.make_async_copy(field_hbm, field_ref, sems.at[0])
-    table_copy = pltpu.make_async_copy(table_hbm, table_ref, sems.at[1])
-    field_copy.start()
+    field_copies = [
+        pltpu.make_async_copy(field_hbm.at[v], field_ref.at[v], sems.at[v]) for v in range(group)
+    ]
+    table_copy = pltpu.make_async_copy(table_hbm, table_ref, sems.at[group])
+    for copy in field_copies:
+        copy.start()
     table_copy.start()
     mirrored = lax.axis_index("grid") >= n_grid // 2
     lane_group = lax.broadcasted_iota(jnp.int32, (blocks * slab, LANES), 1) // size
-    field_copy.wait()
+    for copy in field_copies:
+        copy.wait()
     stacked = [
         jnp.concatenate([field_ref[v, :, b * LANES : (b + 1) * LANES] for b in range(blocks)], 0)
         for v in range(group)
@@ -109,12 +114,20 @@
     values = lax.dot_general(
         table, operand, (((1,), (1,)), ((), ())), preferred_element_type=jnp.float32
     )
-    for parity in range(2):
-        part = values[:, parity * LANES : (parity + 1) * LANES]
-        out_ref[:, parity] = part.reshape(size, 2 * group, LANES)
-    out_copy = pltpu.make_async_copy(out_ref, out_hbm, sems.at[2])
-    out_copy.start()
-    out_copy.wait()
+    parts = sems.shape[0] - group - 1
+    step = size // parts
+    out_copies = []
+    for p in range(parts):
+        rows = slice(p * step * 2 * group, (p + 1) * step * 2 * group)
+        own = slice(p * step, (p + 1) * step)
+        for parity in range(2):
+            part = values[rows, parity * LANES : (parity + 1) * LANES]
+            out_ref[own, parity] = part.reshape(step, 2 * group, LANES)
+        copy = pltpu.make_async_copy(out_ref.at[own], out_hbm.at[own], sems.at[group + 1 + p])
+        copy.start()
+        out_copies.append(copy)
+    for copy in out_copies:
+        copy.wait()
 
 
 def operator_kernel(size, spectrum_ref, cos_ref, wave_ref, turn_ref, high_ref, low_ref):
@@ -198,12 +211,16 @@
         turned = jnp.where(place < n_vec - step, ahead, behind)
         gram = jnp.where(owner // step % 2 == 1, turned, gram)
         step *= 2
+    for v in range(group):
+        out_ref[pl.ds(v, n_vec, stride=group), :] = gram[v * n_vec : (v + 1) * n_vec]
+
+
+def finish_kernel(n_vec, got_ref, out_ref):
+    _, group, shifts = out_ref.shape
+    summed = jnp.sum(got_ref[...], 0, keepdims=True)
     for w in range(group):
-        turned = pltpu.roll(gram, LANES - w * n_vec, 1) if w else gram
-        for v in range(group):
-            out_ref[pl.ds(v * group + w, n_vec, stride=group * group), :] = turned[
-                v * n_vec : (v + 1) * n_vec
-            ]
+        turned = pltpu.roll(summed, LANES - w * n_vec, 1) if w else summed
+        out_ref[0, w : w + 1, :] = turned[:, :shifts]
 
 
 def whole_blocks(count):
@@ -231,7 +248,7 @@
             pltpu.VMEM(table.shape, table.dtype),
             pltpu.VMEM((2, half * slab, LANES), jnp.float32),
             pltpu.VMEM(chunk_shape, jnp.float32),
-            pltpu.SemaphoreType.DMA((3,)),
+            pltpu.SemaphoreType.DMA((group + 1 + OUT_COPIES,)),
         ],
         compiler_params=ALL_VMEM,
         name="analyse",
@@ -267,14 +284,21 @@
 
     rows = pl.pallas_call(
         functools.partial(gram_kernel, n_vec, n_grid, group),
-        out_shape=jax.ShapeDtypeStruct((total * group, LANES), jnp.float32),
+        out_shape=jax.ShapeDtypeStruct((total, LANES), jnp.float32),
         in_specs=whole_blocks(3),
         out_specs=whole_blocks(1)[0],
         compiler_params=PARAMS,
         name="gram",
     )(got.reshape(n_devices * 4 * group, LANES), op_high, op_low)
-    parts = lax.all_to_all(rows.reshape(total, group, LANES), AXES, 0, 0, tiled=True)
-    return jnp.sum(parts[:, :, :shifts], 0).T[None]
+    parts = lax.all_to_all(rows, AXES, 0, 0, tiled=True)
+    return pl.pallas_call(
+        functools.partial(finish_kernel, n_vec),
+        out_shape=jax.ShapeDtypeStruct((1, group, shifts), jnp.float32),
+        in_specs=whole_blocks(1),
+        out_specs=whole_blocks(1)[0],
+        compiler_params=PARAMS,
+        name="finish",
+    )(parts).transpose(0, 2, 1)
 
 
 def general_program(fitting_vectors, size, n_vec, n_grid, shifts):

time: 31.6 us -> 31.3 us (level)
  other arithmetic: 1.02 us -> 0.4 us
  Pallas kernels: 4.36 us -> 4.84 us
    pallas_call x0 -> x1, Pallas kernels: none -> 0.66 us  [tiled_program(): pl.pallas_call(functools.partial(finish_kernel, n_vec), out_shape=jax.Sha...]
    reduce_sum x1 -> x0, other arithmetic: 0.62 us -> none  [tiled_program(): return jnp.sum(parts[:, :, :shifts], 0).T[None]]
where the time goes in v4:
time: 31.3 us; the launch traced here: 30.9 us
  blocking collectives  9.36 us (30%)
  waiting for transfers between devices  8.47 us (27%)
  starting transfers between devices  7.3 us (23%)
  Pallas kernels  4.84 us (15%)
  local copies, waits for them, and re-layouts  0.46 us (1%)
  other arithmetic  0.4 us (1%)
    all_to_all x1, blocking collectives, tiled_program(): parts = lax.all_to_all(rows, AXES, 0, 0, tiled=True)  9.36 us
    all_to_all x1, waiting for transfers between devices, tiled_program(): got = lax.all_to_all(components, AXES, 0, 0, tiled=True)  8.47 us
    all_to_all x1, starting transfers between devices, tiled_program(): got = lax.all_to_all(components, AXES, 0, 0, tiled=True)  7.3 us
    pallas_call x1, Pallas kernels, tiled_program(): pl.pallas_call(functools.partial(analyse_kernel, size, n_grid), out_shape...  2 us
    pallas_call x1, Pallas kernels, tiled_program(): pl.pallas_call(functools.partial(operator_kernel, size), out_shape=(op_sh...  1.22 us
    pallas_call x1, Pallas kernels, tiled_program(): pl.pallas_call(functools.partial(gram_kernel, n_vec, n_grid, group), out_...  0.96 us
    pallas_call x1, Pallas kernels, tiled_program(): pl.pallas_call(functools.partial(finish_kernel, n_vec), out_shape=jax.Sha...  0.66 us
  transfers between devices with their start and end apart: 1, of which 1 were waited for; matrix products, arithmetic and copies ran while one was open for 1% of the time, Pallas kernels for 4%

profile of v4, /device:TPU:0, one launch (start us, length us, event | category | flops | bytes accessed | tf_op | source)
XLA Modules:
  0.0 30.9 jit_solution(15940826247158616288)
XLA Ops:
  0.0 2.0 %analyse.1 = f32[32,2,8,128]{3,2,1,0:T(8,128)} custom-call(f32[4,8,1024]{2,1,0:T(8,128)} %field_hbm.1, bf16[256,256]{1,0:T(8,128)(2,1)} %constant.45.clone.table_hbm), custom_call_target="tpu_custom_call" | custom-call | tf_op jit(solution)/shard_map/analyse/pallas_call | solution.py:241
  2.0 0.0 copy-start
  2.0 0.0 copy-start.1
  2.0 7.3 %all-to-all-start = ((f32[32,2,8,128]{3,2,1,0:T(8,128)}), f32[32,2,8,128]{3,2,1,0:T(8,128)S(1)}, u32[]{:S(2)}, u32[]{:S(2)}) async-start(f32[32,2,8,128]{3,2,1,0:T(8,128)} %analyse.1), calls=%async_computation | async-start | bytes 524288 | tf_op jit(solution)/shard_map/all_to_all | solution.py:256
  9.4 0.1 fusion.11
  9.5 0.1 broadcast_add_fusion
  9.5 0.0 copy-start.2
  9.5 0.2 fusion.4.spectrum_ref
  9.8 0.0 copy-done
  9.8 0.0 copy-done.1
  9.8 0.4 %copy-done.2 = f32[2,16,40]{2,1,0:T(8,128)S(1)} copy-done((f32[2,16,40]{2,1,0:T(8,128)S(1)}, f32[2,16,40]{2,1,0:T(8,128)}, u32[]{:S(2)}) %copy-start.2) | copy-done | bytes 5144
  10.2 1.2 %operator.1 = (bf16[2,2,2,256,256]{4,3,2,1,0:T(8,128)(2,1)S(1)}, bf16[2,2,2,256,256]{4,3,2,1,0:T(8,128)(2,1)S(1)}) custom-call(f32[2,40,40]{2,1,0:T(8,128)S(1)} %fusion.4.spectrum_ref, f32[40,1024]{1,0:T(8,128)S(1)} %copy-done.1, f32[2,40,1024]{2,1,0:T(8,128)S(1)} %copy-done, f32[2,16,40]{2,1,0:T(8,128)S(1)} %copy-done.2), custom_call_target="tpu_custom_call" | custom-call | tf_op jit(solution)/shard_map/operator/pallas_call | solution.py:271
  11.5 8.5 %all-to-all-done = f32[32,2,8,128]{3,2,1,0:T(8,128)S(1)} async-done(((f32[32,2,8,128]{3,2,1,0:T(8,128)}), f32[32,2,8,128]{3,2,1,0:T(8,128)S(1)}, u32[]{:S(2)}, u32[]{:S(2)}) %all-to-all-start) | async-done | bytes 262176 | tf_op jit(solution)/shard_map/all_to_all | solution.py:256
  19.9 1.0 %gram.1 = f32[32,128]{1,0:T(8,128)S(1)} custom-call(f32[512,128]{1,0:T(8,128)S(1)} %bitcast.8, bf16[2,2,2,256,256]{4,3,2,1,0:T(8,128)(2,1)S(1)} %get-tuple-element.7.high_ref, bf16[2,2,2,256,256]{4,3,2,1,0:T(8,128)(2,1)S(1)} %get-tuple-element.8.low_ref), custom_call_target="tpu_custom_call" | custom-call | tf_op jit(solution)/shard_map/gram/pallas_call | solution.py:285
  20.9 9.4 %all_to_all.16 = f32[32,1,128]{2,1,0:T(1,128)S(1)} all-to-all(f32[32,1,128]{2,1,0:T(1,128)S(1)} %bitcast.9), channel_id=1, replica_groups=mesh['vec'=8,'grid'=4] {'vec','grid'}, dimensions={0} | all-to-all | bytes 32768 | tf_op jit(solution)/shard_map/all_to_all | solution.py:293
  30.3 0.7 %finish.1 = f32[1,4,5]{2,1,0:T(4,128)} custom-call(f32[32,128]{1,0:T(8,128)S(1)} %bitcast.10), custom_call_target="tpu_custom_call" | custom-call | tf_op jit(solution)/shard_map/finish/pallas_call | solution.py:294
  (1 shorter events, 0.0 us)
Async XLA Ops:
  2.0 7.8 %copy-start = (f32[2,40,1024]{2,1,0:T(8,128)S(1)}, f32[2,40,1024]{2,1,0:T(8,128)}, u32[]{:S(2)}) copy-start(f32[2,40,1024]{2,1,0:T(8,128)} %constant.47.clone.wave_ref) | copy-start | bytes 983044
  2.0 7.8 %copy-start.1 = (f32[40,1024]{1,0:T(8,128)S(1)}, f32[40,1024]{1,0:T(8,128)}, u32[]{:S(2)}) copy-start(f32[40,1024]{1,0:T(8,128)} %constant.46.clone.cos_ref) | copy-start | bytes 491524
  2.0 17.9 %all-to-all-start = ((f32[32,2,8,128]{3,2,1,0:T(8,128)}), f32[32,2,8,128]{3,2,1,0:T(8,128)S(1)}, u32[]{:S(2)}, u32[]{:S(2)}) async-start(f32[32,2,8,128]{3,2,1,0:T(8,128)} %analyse.1), calls=%async_computation | async-start | bytes 524288 | tf_op jit(solution)/shard_map/all_to_all | solution.py:256
  9.5 0.7 %copy-start.2 = (f32[2,16,40]{2,1,0:T(8,128)S(1)}, f32[2,16,40]{2,1,0:T(8,128)}, u32[]{:S(2)}) copy-start(f32[2,16,40]{2,1,0:T(8,128)} %constant.48.clone.turn_ref) | copy-start | bytes 15364

commit v5 on v4

--- a/solution.py
+++ b/solution.py
@@ -201,26 +201,25 @@
     )
     gram = gram[:total] + gram[total:]
     gram = jnp.concatenate([gram, jnp.zeros((total, LANES - 2 * total), jnp.float32)], 1)
-    gram += pltpu.roll(gram, LANES - total, 1)
-    owner = lax.broadcasted_iota(jnp.int32, gram.shape, 0) % n_vec
-    place = lax.broadcasted_iota(jnp.int32, gram.shape, 1) % n_vec
-    step = 1
-    while step < n_vec:
-        ahead = pltpu.roll(gram, LANES - step, 1)
-        behind = pltpu.roll(gram, n_vec - step, 1)
-        turned = jnp.where(place < n_vec - step, ahead, behind)
-        gram = jnp.where(owner // step % 2 == 1, turned, gram)
-        step *= 2
     for v in range(group):
         out_ref[pl.ds(v, n_vec, stride=group), :] = gram[v * n_vec : (v + 1) * n_vec]
 
 
 def finish_kernel(n_vec, got_ref, out_ref):
     _, group, shifts = out_ref.shape
+    total = n_vec * group
+    g = lax.axis_index("vec")
     summed = jnp.sum(got_ref[...], 0, keepdims=True)
+    lane = lax.broadcasted_iota(jnp.int32, summed.shape, 1)
+
+    def from_lane(first):
+        return pltpu.roll(summed, lax.rem(2 * LANES - first, LANES), 1)
+
     for w in range(group):
-        turned = pltpu.roll(summed, LANES - w * n_vec, 1) if w else summed
-        out_ref[0, w : w + 1, :] = turned[:, :shifts]
+        start = w * n_vec + g
+        ahead = from_lane(start) + from_lane(start + total)
+        behind = from_lane(start - n_vec) + from_lane(start - n_vec + total)
+        out_ref[0, w : w + 1, :] = jnp.where(lane < n_vec - g, ahead, behind)[:, :shifts]
 
 
 def whole_blocks(count):

time: 31.3 us -> 31 us (level)
  no operation moved by 1% of the time
where the time goes in v5:
time: 31 us; the launch traced here: 30.7 us
  blocking collectives  9.36 us (30%)
  waiting for transfers between devices  8.47 us (27%)
  starting transfers between devices  7.3 us (24%)
  Pallas kernels  4.57 us (15%)
  local copies, waits for them, and re-layouts  0.46 us (1%)
  other arithmetic  0.4 us (1%)
    all_to_all x1, blocking collectives, tiled_program(): parts = lax.all_to_all(rows, AXES, 0, 0, tiled=True)  9.36 us
    all_to_all x1, waiting for transfers between devices, tiled_program(): got = lax.all_to_all(components, AXES, 0, 0, tiled=True)  8.47 us
    all_to_all x1, starting transfers between devices, tiled_program(): got = lax.all_to_all(components, AXES, 0, 0, tiled=True)  7.3 us
    pallas_call x1, Pallas kernels, tiled_program(): pl.pallas_call(functools.partial(analyse_kernel, size, n_grid), out_shape...  2 us
    pallas_call x1, Pallas kernels, tiled_program(): pl.pallas_call(functools.partial(operator_kernel, size), out_shape=(op_sh...  1.22 us
    pallas_call x1, Pallas kernels, tiled_program(): pl.pallas_call(functools.partial(gram_kernel, n_vec, n_grid, group), out_...  0.68 us
    pallas_call x1, Pallas kernels, tiled_program(): pl.pallas_call(functools.partial(finish_kernel, n_vec), out_shape=jax.Sha...  0.67 us
  transfers between devices with their start and end apart: 1, of which 1 were waited for; matrix products, arithmetic and copies ran while one was open for 1% of the time, Pallas kernels for 4%

profile of v5, /device:TPU:0, one launch (start us, length us, event | category | flops | bytes accessed | tf_op | source)
XLA Modules:
  0.0 30.7 jit_solution(3094639471179311029)
XLA Ops:
  0.0 2.0 %analyse.1 = f32[32,2,8,128]{3,2,1,0:T(8,128)} custom-call(f32[4,8,1024]{2,1,0:T(8,128)} %field_hbm.1, bf16[256,256]{1,0:T(8,128)(2,1)} %constant.45.clone.table_hbm), custom_call_target="tpu_custom_call" | custom-call | tf_op jit(solution)/shard_map/analyse/pallas_call | solution.py:240
  2.0 0.0 copy-start
  2.0 0.0 copy-start.1
  2.0 7.3 %all-to-all-start = ((f32[32,2,8,128]{3,2,1,0:T(8,128)}), f32[32,2,8,128]{3,2,1,0:T(8,128)S(1)}, u32[]{:S(2)}, u32[]{:S(2)}) async-start(f32[32,2,8,128]{3,2,1,0:T(8,128)} %analyse.1), calls=%async_computation | async-start | bytes 524288 | tf_op jit(solution)/shard_map/all_to_all | solution.py:255
  9.4 0.1 fusion.11
  9.5 0.1 broadcast_add_fusion
  9.5 0.0 copy-start.2
  9.5 0.2 fusion.4.spectrum_ref
  9.8 0.0 copy-done
  9.8 0.0 copy-done.1
  9.8 0.4 %copy-done.2 = f32[2,16,40]{2,1,0:T(8,128)S(1)} copy-done((f32[2,16,40]{2,1,0:T(8,128)S(1)}, f32[2,16,40]{2,1,0:T(8,128)}, u32[]{:S(2)}) %copy-start.2) | copy-done | bytes 5144
  10.2 1.2 %operator.1 = (bf16[2,2,2,256,256]{4,3,2,1,0:T(8,128)(2,1)S(1)}, bf16[2,2,2,256,256]{4,3,2,1,0:T(8,128)(2,1)S(1)}) custom-call(f32[2,40,40]{2,1,0:T(8,128)S(1)} %fusion.4.spectrum_ref, f32[40,1024]{1,0:T(8,128)S(1)} %copy-done.1, f32[2,40,1024]{2,1,0:T(8,128)S(1)} %copy-done, f32[2,16,40]{2,1,0:T(8,128)S(1)} %copy-done.2), custom_call_target="tpu_custom_call" | custom-call | tf_op jit(solution)/shard_map/operator/pallas_call | solution.py:270
  11.5 8.5 %all-to-all-done = f32[32,2,8,128]{3,2,1,0:T(8,128)S(1)} async-done(((f32[32,2,8,128]{3,2,1,0:T(8,128)}), f32[32,2,8,128]{3,2,1,0:T(8,128)S(1)}, u32[]{:S(2)}, u32[]{:S(2)}) %all-to-all-start) | async-done | bytes 262176 | tf_op jit(solution)/shard_map/all_to_all | solution.py:255
  19.9 0.7 %gram.1 = f32[32,128]{1,0:T(8,128)S(1)} custom-call(f32[512,128]{1,0:T(8,128)S(1)} %bitcast.8, bf16[2,2,2,256,256]{4,3,2,1,0:T(8,128)(2,1)S(1)} %get-tuple-element.7.high_ref, bf16[2,2,2,256,256]{4,3,2,1,0:T(8,128)(2,1)S(1)} %get-tuple-element.8.low_ref), custom_call_target="tpu_custom_call" | custom-call | tf_op jit(solution)/shard_map/gram/pallas_call | solution.py:284
  20.6 9.4 %all_to_all.16 = f32[32,1,128]{2,1,0:T(1,128)S(1)} all-to-all(f32[32,1,128]{2,1,0:T(1,128)S(1)} %bitcast.9), channel_id=1, replica_groups=mesh['vec'=8,'grid'=4] {'vec','grid'}, dimensions={0} | all-to-all | bytes 32768 | tf_op jit(solution)/shard_map/all_to_all | solution.py:292
  30.0 0.7 %finish.1 = f32[1,4,5]{2,1,0:T(4,128)} custom-call(f32[32,128]{1,0:T(8,128)S(1)} %bitcast.10), custom_call_target="tpu_custom_call" | custom-call | tf_op jit(solution)/shard_map/finish/pallas_call | solution.py:293
  (1 shorter events, 0.0 us)
Async XLA Ops:
  2.0 7.8 %copy-start = (f32[2,40,1024]{2,1,0:T(8,128)S(1)}, f32[2,40,1024]{2,1,0:T(8,128)}, u32[]{:S(2)}) copy-start(f32[2,40,1024]{2,1,0:T(8,128)} %constant.47.clone.wave_ref) | copy-start | bytes 983044
  2.0 7.8 %copy-start.1 = (f32[40,1024]{1,0:T(8,128)S(1)}, f32[40,1024]{1,0:T(8,128)}, u32[]{:S(2)}) copy-start(f32[40,1024]{1,0:T(8,128)} %constant.46.clone.cos_ref) | copy-start | bytes 491524
  2.0 17.9 %all-to-all-start = ((f32[32,2,8,128]{3,2,1,0:T(8,128)}), f32[32,2,8,128]{3,2,1,0:T(8,128)S(1)}, u32[]{:S(2)}, u32[]{:S(2)}) async-start(f32[32,2,8,128]{3,2,1,0:T(8,128)} %analyse.1), calls=%async_computation | async-start | bytes 524288 | tf_op jit(solution)/shard_map/all_to_all | solution.py:255
  9.5 0.7 %copy-start.2 = (f32[2,16,40]{2,1,0:T(8,128)S(1)}, f32[2,16,40]{2,1,0:T(8,128)}, u32[]{:S(2)}) copy-start(f32[2,16,40]{2,1,0:T(8,128)} %constant.48.clone.turn_ref) | copy-start | bytes 15364

commit v6 on v5

--- a/solution.py
+++ b/solution.py
@@ -167,15 +167,23 @@
     total = n_vec * group
     tile = 2 * group
 
-    left, right = [], []
-    for c in range(2):
+    def apply(high, low, which):
+        op_high, op_low = high_ref[which], low_ref[which]
+        both = jnp.dot(
+            jnp.concatenate([high, low], 0), op_high, preferred_element_type=jnp.float32
+        )
+        applied = both[: high.shape[0]] + both[high.shape[0] :]
+        return applied + jnp.dot(high, op_low, preferred_element_type=jnp.float32)
+
+    def gram_rows(one_operator):
+        left, right = [], []
         for parity in range(2):
             slabs = []
             for i in range(n_grid):
-                start = (i * 2 + parity) * tile + c * group
+                start = (i * 2 + parity) * tile
                 rows = [
-                    got_ref[pl.ds(start + v, n_vec, stride=n_grid * 2 * tile), :]
-                    for v in range(group)
+                    got_ref[pl.ds(start + row, n_vec, stride=n_grid * 2 * tile), :]
+                    for row in range(tile)
                 ]
                 slabs.append(jnp.concatenate(rows, 0))
             for sign in range(2):
@@ -183,26 +191,38 @@
                 for i in range(n_grid // 2):
                     near, far = slabs[i], slabs[n_grid - 1 - i]
                     folded.append(near - far if sign else near + far)
-                value = jnp.concatenate(folded, 1)
-                high, low = split_bf16(value)
-                op_high, op_low = high_ref[c, parity, sign], low_ref[c, parity, sign]
-                both = jnp.dot(
-                    jnp.concatenate([high, low], 0), op_high, preferred_element_type=jnp.float32
-                )
-                applied = both[:total] + both[total:]
-                applied += jnp.dot(high, op_low, preferred_element_type=jnp.float32)
-                left.append(jnp.concatenate(split_bf16(applied), 0))
-                right.append(jnp.concatenate([high, low], 0))
-    gram = lax.dot_general(
-        jnp.concatenate(left, 1),
-        jnp.concatenate(right, 1),
-        (((1,), (1,)), ((), ())),
-        preferred_element_type=jnp.float32,
-    )
-    gram = gram[:total] + gram[total:]
-    gram = jnp.concatenate([gram, jnp.zeros((total, LANES - 2 * total), jnp.float32)], 1)
-    for v in range(group):
-        out_ref[pl.ds(v, n_vec, stride=group), :] = gram[v * n_vec : (v + 1) * n_vec]
+                high, low = split_bf16(jnp.concatenate(folded, 1))
+                own = [slice(c * total, (c + 1) * total) for c in range(2)]
+                if one_operator:
+                    applied = apply(high, low, (0, parity, sign))
+                else:
+                    applied = jnp.concatenate(
+                        [apply(high[own[c]], low[own[c]], (c, parity, sign)) for c in range(2)], 0
+                    )
+                applied_high, applied_low = split_bf16(applied)
+                for rows in own:
+                    left.append(jnp.concatenate([applied_high[rows], applied_low[rows]], 0))
+                    right.append(jnp.concatenate([high[rows], low[rows]], 0))
+        gram = lax.dot_general(
+            jnp.concatenate(left, 1),
+            jnp.concatenate(right, 1),
+            (((1,), (1,)), ((), ())),
+            preferred_element_type=jnp.float32,
+        )
+        gram = gram[:total] + gram[total:]
+        gram = jnp.concatenate([gram, jnp.zeros((total, LANES - 2 * total), jnp.float32)], 1)
+        for v in range(group):
+            out_ref[pl.ds(v, n_vec, stride=group), :] = gram[v * n_vec : (v + 1) * n_vec]
+
+    first = (lax.axis_index("vec") == 0) & (lax.axis_index("grid") == 0)
+
+    @pl.when(first)
+    def _():
+        gram_rows(False)
+
+    @pl.when(jnp.logical_not(first))
+    def _():
+        gram_rows(True)
 
 
 def finish_kernel(n_vec, got_ref, out_ref):

time: 31 us -> 30.9 us (level)
  no operation moved by 1% of the time
where the time goes in v6:
time: 30.9 us; the launch traced here: 30.5 us
  blocking collectives  9.25 us (30%)
  waiting for transfers between devices  8.47 us (27%)
  starting transfers between devices  7.3 us (24%)
  Pallas kernels  4.56 us (15%)
  local copies, waits for them, and re-layouts  0.46 us (1%)
  other arithmetic  0.4 us (1%)
    all_to_all x1, blocking collectives, tiled_program(): parts = lax.all_to_all(rows, AXES, 0, 0, tiled=True)  9.25 us
    all_to_all x1, waiting for transfers between devices, tiled_program(): got = lax.all_to_all(components, AXES, 0, 0, tiled=True)  8.47 us
    all_to_all x1, starting transfers between devices, tiled_program(): got = lax.all_to_all(components, AXES, 0, 0, tiled=True)  7.3 us
    pallas_call x1, Pallas kernels, tiled_program(): pl.pallas_call(functools.partial(analyse_kernel, size, n_grid), out_shape...  2 us
    pallas_call x1, Pallas kernels, tiled_program(): pl.pallas_call(functools.partial(operator_kernel, size), out_shape=(op_sh...  1.22 us
    pallas_call x1, Pallas kernels, tiled_program(): pl.pallas_call(functools.partial(gram_kernel, n_vec, n_grid, group), out_...  0.67 us
    pallas_call x1, Pallas kernels, tiled_program(): pl.pallas_call(functools.partial(finish_kernel, n_vec), out_shape=jax.Sha...  0.67 us
  transfers between devices with their start and end apart: 1, of which 1 were waited for; matrix products, arithmetic and copies ran while one was open for 1% of the time, Pallas kernels for 4%

profile of v6, /device:TPU:0, one launch (start us, length us, event | category | flops | bytes accessed | tf_op | source)
XLA Modules:
  0.0 30.5 jit_solution(6229347411585784688)
XLA Ops:
  0.0 2.0 %analyse.1 = f32[32,2,8,128]{3,2,1,0:T(8,128)} custom-call(f32[4,8,1024]{2,1,0:T(8,128)} %field_hbm.1, bf16[256,256]{1,0:T(8,128)(2,1)} %constant.45.clone.table_hbm), custom_call_target="tpu_custom_call" | custom-call | tf_op jit(solution)/shard_map/analyse/pallas_call | solution.py:260
  2.0 0.0 copy-start
  2.0 0.0 copy-start.1
  2.0 7.3 %all-to-all-start = ((f32[32,2,8,128]{3,2,1,0:T(8,128)}), f32[32,2,8,128]{3,2,1,0:T(8,128)S(1)}, u32[]{:S(2)}, u32[]{:S(2)}) async-start(f32[32,2,8,128]{3,2,1,0:T(8,128)} %analyse.1), calls=%async_computation | async-start | bytes 524288 | tf_op jit(solution)/shard_map/all_to_all | solution.py:275
  9.4 0.1 fusion.11
  9.5 0.1 broadcast_add_fusion
  9.5 0.0 copy-start.2
  9.5 0.2 fusion.4.spectrum_ref
  9.8 0.0 copy-done
  9.8 0.0 copy-done.1
  9.8 0.4 %copy-done.2 = f32[2,16,40]{2,1,0:T(8,128)S(1)} copy-done((f32[2,16,40]{2,1,0:T(8,128)S(1)}, f32[2,16,40]{2,1,0:T(8,128)}, u32[]{:S(2)}) %copy-start.2) | copy-done | bytes 5144
  10.2 1.2 %operator.1 = (bf16[2,2,2,256,256]{4,3,2,1,0:T(8,128)(2,1)S(1)}, bf16[2,2,2,256,256]{4,3,2,1,0:T(8,128)(2,1)S(1)}) custom-call(f32[2,40,40]{2,1,0:T(8,128)S(1)} %fusion.4.spectrum_ref, f32[40,1024]{1,0:T(8,128)S(1)} %copy-done.1, f32[2,40,1024]{2,1,0:T(8,128)S(1)} %copy-done, f32[2,16,40]{2,1,0:T(8,128)S(1)} %copy-done.2), custom_call_target="tpu_custom_call" | custom-call | tf_op jit(solution)/shard_map/operator/pallas_call | solution.py:290
  11.5 8.5 %all-to-all-done = f32[32,2,8,128]{3,2,1,0:T(8,128)S(1)} async-done(((f32[32,2,8,128]{3,2,1,0:T(8,128)}), f32[32,2,8,128]{3,2,1,0:T(8,128)S(1)}, u32[]{:S(2)}, u32[]{:S(2)}) %all-to-all-start) | async-done | bytes 262176 | tf_op jit(solution)/shard_map/all_to_all | solution.py:275
  19.9 0.7 %gram.1 = f32[32,128]{1,0:T(8,128)S(1)} custom-call(f32[512,128]{1,0:T(8,128)S(1)} %bitcast.8, bf16[2,2,2,256,256]{4,3,2,1,0:T(8,128)(2,1)S(1)} %get-tuple-element.7.high_ref, bf16[2,2,2,256,256]{4,3,2,1,0:T(8,128)(2,1)S(1)} %get-tuple-element.8.low_ref), custom_call_target="tpu_custom_call" | custom-call | tf_op jit(solution)/shard_map/gram/pallas_call | solution.py:304
  20.6 9.2 %all_to_all.16 = f32[32,1,128]{2,1,0:T(1,128)S(1)} all-to-all(f32[32,1,128]{2,1,0:T(1,128)S(1)} %bitcast.9), channel_id=1, replica_groups=mesh['vec'=8,'grid'=4] {'vec','grid'}, dimensions={0} | all-to-all | bytes 32768 | tf_op jit(solution)/shard_map/all_to_all | solution.py:312
  29.9 0.7 %finish.1 = f32[1,4,5]{2,1,0:T(4,128)} custom-call(f32[32,128]{1,0:T(8,128)S(1)} %bitcast.10), custom_call_target="tpu_custom_call" | custom-call | tf_op jit(solution)/shard_map/finish/pallas_call | solution.py:313
  (1 shorter events, 0.0 us)
Async XLA Ops:
  2.0 7.8 %copy-start = (f32[2,40,1024]{2,1,0:T(8,128)S(1)}, f32[2,40,1024]{2,1,0:T(8,128)}, u32[]{:S(2)}) copy-start(f32[2,40,1024]{2,1,0:T(8,128)} %constant.47.clone.wave_ref) | copy-start | bytes 983044
  2.0 7.8 %copy-start.1 = (f32[40,1024]{1,0:T(8,128)S(1)}, f32[40,1024]{1,0:T(8,128)}, u32[]{:S(2)}) copy-start(f32[40,1024]{1,0:T(8,128)} %constant.46.clone.cos_ref) | copy-start | bytes 491524
  2.0 17.9 %all-to-all-start = ((f32[32,2,8,128]{3,2,1,0:T(8,128)}), f32[32,2,8,128]{3,2,1,0:T(8,128)S(1)}, u32[]{:S(2)}, u32[]{:S(2)}) async-start(f32[32,2,8,128]{3,2,1,0:T(8,128)} %analyse.1), calls=%async_computation | async-start | bytes 524288 | tf_op jit(solution)/shard_map/all_to_all | solution.py:275
  9.5 0.7 %copy-start.2 = (f32[2,16,40]{2,1,0:T(8,128)S(1)}, f32[2,16,40]{2,1,0:T(8,128)}, u32[]{:S(2)}) copy-start(f32[2,16,40]{2,1,0:T(8,128)} %constant.48.clone.turn_ref) | copy-start | bytes 15364

commit v7 on v6

--- a/solution.py
+++ b/solution.py
@@ -12,9 +12,7 @@
 AXES = ("vec", "grid")
 LANES = 128
 ROWS = 8
-OUT_COPIES = 4
 PARAMS = pltpu.CompilerParams(vmem_limit_bytes=16 * 2**20)
-ALL_VMEM = pltpu.CompilerParams(vmem_limit_bytes=60 * 2**20)
 
 
 def centred(size):
@@ -33,25 +31,39 @@
     return np.where(np.isin(np.arange(size + 1), (0, size)), 1.0, 2.0)
 
 
-def operator_spectrum(size, pair, kx_pad=0, ky_pad=0):
-    kz = jnp.stack([pair, jnp.where(pair == 0, size, pair)]).astype(jnp.float32)
-    times = jnp.where(pair == 0, 1.0, 2.0)
-    ky = jnp.arange(size + 1 + ky_pad, dtype=jnp.int32)
-    kx = jnp.arange(size + 1 + kx_pad, dtype=jnp.int32)
-    fy, fx = ky.astype(jnp.float32), kx.astype(jnp.float32)
-    total_sq = (kz * kz)[:, None, None] + (fy * fy)[None, :, None] + (fx * fx)[None, None, :]
+def kernel_values(size, kz, ky, kx):
+    total_sq = kz * kz + ky * ky + kx * kx
     wave_sq = total_sq * (math.pi / size) ** 2
     safe_sq = jnp.where(total_sq > 0, wave_sq, 1.0)
     half_arg = 0.5 * jnp.sqrt(safe_sq) * size
     values = 8.0 * math.pi * jnp.sin(half_arg) ** 2 / safe_sq
-    values = jnp.where(total_sq > 0, values, 2.0 * math.pi * size * size)
-
-    def weight(k):
-        inside = jnp.where((k == 0) | (k == size), 1.0, 2.0)
-        return jnp.where(k <= size, inside, 0.0)
-
-    scale = times / (float(2 * size) ** 3 * float(size) ** 3)
-    return values * weight(ky)[None, :, None] * weight(kx)[None, None, :] * scale
+    return jnp.where(total_sq > 0, values, 2.0 * math.pi * size * size)
+
+
+def times(size, k):
+    inside = jnp.where((k == 0) | (k == size), 1.0, 2.0)
+    return jnp.where(k <= size, inside, 0.0)
+
+
+def scaled(size, values, pair, ky, kx):
+    scale = 1.0 / (float(2 * size) ** 3 * float(size) ** 3)
+    return values * times(size, ky) * times(size, kx) * jnp.where(pair == 0, scale, 2.0 * scale)
+
+
+def operator_spectrum(size, pair, c, n_ky):
+    ky = lax.broadcasted_iota(jnp.int32, (n_ky, LANES), 0)
+    kx = lax.broadcasted_iota(jnp.int32, (n_ky, LANES), 1)
+    kz = jnp.where(pair == 0, size, pair) if c else pair
+    fz, fy, fx = (k.astype(jnp.float32) for k in (kz, ky, kx))
+    return scaled(size, kernel_values(size, fz, fy, fx), pair, ky, kx)
+
+
+def pair_spectrum(size, pair):
+    kz = jnp.stack([pair, jnp.where(pair == 0, size, pair)])[:, None, None]
+    ky = jnp.arange(size + 1, dtype=jnp.int32)[None, :, None]
+    kx = jnp.arange(size + 1, dtype=jnp.int32)[None, None, :]
+    fz, fy, fx = (k.astype(jnp.float32) for k in (kz, ky, kx))
+    return scaled(size, kernel_values(size, fz, fy, fx), pair, ky, kx)
 
 
 def split_bf16(value):
@@ -65,8 +77,24 @@
     return high, (table - high.astype(np.float32)).astype(jnp.bfloat16)
 
 
-def analyse_kernel(
-    size, n_grid, field_hbm, table_hbm, out_hbm, field_ref, table_ref, held_ref, out_ref, sems
+def prepare_kernel(
+    size,
+    n_grid,
+    field_hbm,
+    table_hbm,
+    cos_hbm,
+    wave_hbm,
+    turn_hbm,
+    out_ref,
+    high_ref,
+    low_ref,
+    field_ref,
+    table_ref,
+    cos_ref,
+    wave_ref,
+    turn_ref,
+    held_ref,
+    sems,
 ):
     group, slab, _ = field_ref.shape
     half = size // 2
@@ -75,10 +103,16 @@
     field_copies = [
         pltpu.make_async_copy(field_hbm.at[v], field_ref.at[v], sems.at[v]) for v in range(group)
     ]
-    table_copy = pltpu.make_async_copy(table_hbm, table_ref, sems.at[group])
-    for copy in field_copies:
+    pairs = ((table_hbm, table_ref), (cos_hbm, cos_ref), (wave_hbm, wave_ref), (turn_hbm, turn_ref))
+    table_copies = [
+        pltpu.make_async_copy(source, target, sems.at[group + t])
+        for t, (source, target) in enumerate(pairs)
+    ]
+    for copy in field_copies + table_copies:
         copy.start()
-    table_copy.start()
+    n_ky = wave_ref.shape[1]
+    pair = lax.axis_index("vec") * n_grid + lax.axis_index("grid")
+    spectrum = operator_spectrum(size, pair, 0, n_ky)
     mirrored = lax.axis_index("grid") >= n_grid // 2
     lane_group = lax.broadcasted_iota(jnp.int32, (blocks * slab, LANES), 1) // size
     for copy in field_copies:
@@ -109,42 +143,35 @@
             rows.append(held_ref[parity, pl.ds(start, half, stride=slab), :])
     high, low = split_bf16(jnp.concatenate(rows, 0))
     operand = jnp.concatenate([high, high, low], 1)
-    table_copy.wait()
+    for copy in table_copies:
+        copy.wait()
     table = jnp.concatenate([table_ref[...], table_ref[:, :LANES]], 1)
     values = lax.dot_general(
         table, operand, (((1,), (1,)), ((), ())), preferred_element_type=jnp.float32
     )
-    parts = sems.shape[0] - group - 1
-    step = size // parts
-    out_copies = []
-    for p in range(parts):
-        rows = slice(p * step * 2 * group, (p + 1) * step * 2 * group)
-        own = slice(p * step, (p + 1) * step)
-        for parity in range(2):
-            part = values[rows, parity * LANES : (parity + 1) * LANES]
-            out_ref[own, parity] = part.reshape(step, 2 * group, LANES)
-        copy = pltpu.make_async_copy(out_ref.at[own], out_hbm.at[own], sems.at[group + 1 + p])
-        copy.start()
-        out_copies.append(copy)
-    for copy in out_copies:
-        copy.wait()
-
-
-def operator_kernel(size, spectrum_ref, cos_ref, wave_ref, turn_ref, high_ref, low_ref):
-    half = size // 2
+    for parity in range(2):
+        part = values[:, parity * LANES : (parity + 1) * LANES]
+        out_ref[:, parity] = part.reshape(size, 2 * group, LANES)
+
     width = half * half
     exact = lax.Precision.HIGHEST
-    for c in range(2):
+    spread = [jnp.concatenate([wave_ref[p]] * (cos_ref.shape[1] // LANES), 1) for p in range(2)]
+
+    def build(c, spectrum):
         along = jnp.dot(
-            spectrum_ref[c], cos_ref[...], precision=exact, preferred_element_type=jnp.float32
+            spectrum[:, : cos_ref.shape[0]],
+            cos_ref[...],
+            precision=exact,
+            preferred_element_type=jnp.float32,
+        )
+        strips = jnp.dot(
+            turn_ref[...],
+            jnp.concatenate([along * spread[p] for p in range(2)], 0),
+            precision=exact,
+            preferred_element_type=jnp.float32,
         )
         for parity in range(2):
-            strip = jnp.dot(
-                turn_ref[parity],
-                along * wave_ref[parity],
-                precision=exact,
-                preferred_element_type=jnp.float32,
-            )
+            strip = strips[parity * half : (parity + 1) * half]
 
             def window(start):
                 base = start // LANES * LANES
@@ -161,6 +188,12 @@
                     high, low = split_bf16(value)
                     high_ref[c, parity, sign, x * half : (x + 1) * half, :] = high
                     low_ref[c, parity, sign, x * half : (x + 1) * half, :] = low
+
+    build(0, spectrum)
+
+    @pl.when(pair == 0)
+    def _():
+        build(1, operator_spectrum(size, pair, 1, n_ky))
 
 
 def gram_kernel(n_vec, n_grid, group, got_ref, high_ref, low_ref, out_ref):
@@ -251,56 +284,42 @@
     half = size // 2
     n_devices = n_vec * n_grid
     total = n_vec * group
-    pair = lax.axis_index(AXES)
-
     spread = np.einsum("kcz,vw->kcvwz", pair_table(size), np.eye(group))
     high, low = split_table(spread.reshape(size * 2 * group, group * size))
-    table = jnp.asarray(np.concatenate([high, low], 1))
-    chunk_shape = (size, 2, 2 * group, LANES)
-    components = pl.pallas_call(
-        functools.partial(analyse_kernel, size, n_grid),
-        out_shape=jax.ShapeDtypeStruct(chunk_shape, jnp.float32),
-        in_specs=[pl.BlockSpec(memory_space=pltpu.HBM)] * 2,
-        out_specs=pl.BlockSpec(memory_space=pltpu.HBM),
-        scratch_shapes=[
-            pltpu.VMEM(fitting_vectors.shape, jnp.float32),
-            pltpu.VMEM(table.shape, table.dtype),
-            pltpu.VMEM((2, half * slab, LANES), jnp.float32),
-            pltpu.VMEM(chunk_shape, jnp.float32),
-            pltpu.SemaphoreType.DMA((group + 1 + OUT_COPIES,)),
-        ],
-        compiler_params=ALL_VMEM,
-        name="analyse",
-    )(fitting_vectors, table)
-    got = lax.all_to_all(components, AXES, 0, 0, tiled=True)
-
     omega = math.pi / size
-    ky_pad = -(size + 1) % ROWS
-    kx_pad = -(size + 1) % ROWS
-    spectrum = operator_spectrum(size, pair, kx_pad, ky_pad)
-    freqs_y = np.arange(size + 1 + ky_pad)
-    freqs_x = np.arange(size + 1 + kx_pad)
+    freqs = np.arange(-(-(size + 1) // ROWS) * ROWS)
     offsets = np.arange(-(size - 1), size + 1)
-    cos_table = np.repeat(np.cos(omega * np.outer(freqs_x, offsets)), half, 1)
-    angle = omega * np.outer(freqs_y, centred(size)[:half])
+    angle = omega * np.outer(freqs, centred(size)[:half])
     waves = np.stack([np.cos(angle), np.sin(angle)])
     waves[0, size] = 0.0
     waves[1, 0] = 0.0
+    turn = np.einsum("pky,pq->pyqk", waves, np.eye(2))
+    tables = [
+        np.concatenate([high, low], 1),
+        np.repeat(np.cos(omega * np.outer(freqs, offsets)), half, 1).astype(np.float32),
+        np.tile(waves, (1, 1, LANES // half)).astype(np.float32),
+        turn.reshape(2 * half, 2 * len(freqs)).astype(np.float32),
+    ]
     op_shape = jax.ShapeDtypeStruct((2, 2, 2, half * half, half * half), jnp.bfloat16)
-    op_high, op_low = pl.pallas_call(
-        functools.partial(operator_kernel, size),
-        out_shape=(op_shape, op_shape),
-        in_specs=whole_blocks(4),
-        out_specs=tuple(whole_blocks(2)),
+    arguments = [fitting_vectors] + [jnp.asarray(t) for t in tables]
+    components, op_high, op_low = pl.pallas_call(
+        functools.partial(prepare_kernel, size, n_grid),
+        out_shape=(
+            jax.ShapeDtypeStruct((size, 2, 2 * group, LANES), jnp.float32),
+            op_shape,
+            op_shape,
+        ),
+        in_specs=[pl.BlockSpec(memory_space=pltpu.HBM)] * len(arguments),
+        out_specs=tuple(whole_blocks(3)),
+        scratch_shapes=[pltpu.VMEM(a.shape, a.dtype) for a in arguments]
+        + [
+            pltpu.VMEM((2, half * slab, LANES), jnp.float32),
+            pltpu.SemaphoreType.DMA((group + len(tables),)),
+        ],
         compiler_params=PARAMS,
-        name="operator",
-    )(
-        spectrum,
-        jnp.asarray(cos_table, jnp.float32),
-        jnp.asarray(np.tile(waves, (1, 1, 2 * size)), jnp.float32),
-        jnp.asarray(np.swapaxes(waves, 1, 2), jnp.float32),
-    )
-
+        name="prepare",
+    )(*(pltpu.with_memory_space_constraint(a, pltpu.HBM) for a in arguments))
+    got = lax.all_to_all(components, AXES, 0, 0, tiled=True)
     rows = pl.pallas_call(
         functools.partial(gram_kernel, n_vec, n_grid, group),
         out_shape=jax.ShapeDtypeStruct((total, LANES), jnp.float32),
@@ -349,7 +368,7 @@
     start = rank % sharers * columns
     gram = jnp.zeros((total, total), jnp.float32)
     for h in range(held):
-        spectrum = operator_spectrum(size, rank // sharers * held + h)
+        spectrum = pair_spectrum(size, rank // sharers * held + h)
         along = jnp.einsum("clk,xak->clxa", spectrum, steps, precision=exact)
         operator = jnp.einsum("ybl,clxa->cxyab", steps, along, precision=exact)
         operator = operator.reshape(2, size * size, size * size)

time: 30.9 us -> 30.4 us (0.984)
  blocking collectives: 9.25 us -> 26.1 us
  waiting for transfers between devices: 8.47 us -> 0 us
  starting transfers between devices: 7.3 us -> 0 us
  local copies, waits for them, and re-layouts: 0.46 us -> 0 us
  other arithmetic: 0.4 us -> 0 us
  Pallas kernels: 4.56 us -> 4.2 us
    all_to_all x0 -> x1, blocking collectives: none -> 16.8 us  [tiled_program(): got = lax.all_to_all(components, AXES, 0, 0, tiled=True)]
    all_to_all x1 -> x0, waiting for transfers between devices: 8.47 us -> none  [tiled_program(): got = lax.all_to_all(components, AXES, 0, 0, tiled=True)]
    all_to_all x1 -> x0, starting transfers between devices: 7.3 us -> none  [tiled_program(): got = lax.all_to_all(components, AXES, 0, 0, tiled=True)]
    unnamed x6 -> x0, local copies, waits for them, and re-layouts: 0.46 us -> none
    pallas_call x2 -> x1, Pallas kernels: 3.23 us -> 2.86 us  [tiled_program(): pl.pallas_call(functools.partial(prepare_kernel, size, n_grid), out_shape...]
    mul x2 -> x0, other arithmetic: 0.33 us -> none  [the longest x1 0.25 us: operator_spectrum(): values * weight(ky)[None, :, None] * weight(kx)[None, None, :] * scale]
  transfers between devices with their start and end apart: 1 -> 0, of which waited for: 1 -> 0; matrix products, arithmetic and copies ran while one was open for 1% -> 0% of each run, Pallas kernels for 4% -> 0%
where the time goes in v7:
time: 30.4 us; the launch traced here: 30.3 us
  blocking collectives  26.1 us (86%)
  Pallas kernels  4.2 us (14%)
    all_to_all x1, blocking collectives, tiled_program(): got = lax.all_to_all(components, AXES, 0, 0, tiled=True)  16.8 us
    all_to_all x1, blocking collectives, tiled_program(): parts = lax.all_to_all(rows, AXES, 0, 0, tiled=True)  9.24 us
    pallas_call x1, Pallas kernels, tiled_program(): pl.pallas_call(functools.partial(prepare_kernel, size, n_grid), out_shape...  2.86 us
    pallas_call x1, Pallas kernels, tiled_program(): pl.pallas_call(functools.partial(gram_kernel, n_vec, n_grid, group), out_...  0.67 us
    pallas_call x1, Pallas kernels, tiled_program(): pl.pallas_call(functools.partial(finish_kernel, n_vec), out_shape=jax.Sha...  0.67 us

profile of v7, /device:TPU:0, one launch (start us, length us, event | category | flops | bytes accessed | tf_op | source)
XLA Modules:
  0.0 30.3 jit_solution(11064981841424347182)
XLA Ops:
  0.0 2.9 %prepare.1 = (f32[32,2,8,128]{3,2,1,0:T(8,128)S(1)}, bf16[2,2,2,256,256]{4,3,2,1,0:T(8,128)(2,1)S(1)}, bf16[2,2,2,256,256]{4,3,2,1,0:T(8,128)(2,1)S(1)}) custom-call(f32[4,8,1024]{2,1,0:T(8,128)} %field_hbm.1, bf16[256,256]{1,0:T(8,128)(2,1)} %constant.8.clone.table_hbm, f32[40,1024]{1,0:T(8,128)} %constant.9.clone.cos_hbm, ...), custom_call_target="tpu_custom_call" | custom-call | tf_op jit(solution)/shard_map/prepare/pallas_call | solution.py:305
  2.9 16.8 %all_to_all.16 = f32[32,2,8,128]{3,2,1,0:T(8,128)S(1)} all-to-all(f32[32,2,8,128]{3,2,1,0:T(8,128)S(1)} %get-tuple-element.8), channel_id=1, replica_groups=mesh['vec'=8,'grid'=4] {'vec','grid'}, dimensions={0} | all-to-all | bytes 524288 | tf_op jit(solution)/shard_map/all_to_all | solution.py:322
  19.7 0.7 %gram.1 = f32[32,128]{1,0:T(8,128)S(1)} custom-call(f32[512,128]{1,0:T(8,128)S(1)} %bitcast.6, bf16[2,2,2,256,256]{4,3,2,1,0:T(8,128)(2,1)S(1)} %get-tuple-element.9.high_ref, bf16[2,2,2,256,256]{4,3,2,1,0:T(8,128)(2,1)S(1)} %get-tuple-element.10.low_ref), custom_call_target="tpu_custom_call" | custom-call | tf_op jit(solution)/shard_map/gram/pallas_call | solution.py:323
  20.3 9.2 %all_to_all.17 = f32[32,1,128]{2,1,0:T(1,128)S(1)} all-to-all(f32[32,1,128]{2,1,0:T(1,128)S(1)} %bitcast.7), channel_id=1, replica_groups=mesh['vec'=8,'grid'=4] {'vec','grid'}, dimensions={0} | all-to-all | bytes 32768 | tf_op jit(solution)/shard_map/all_to_all | solution.py:331
  29.6 0.7 %finish.1 = f32[1,4,5]{2,1,0:T(4,128)} custom-call(f32[32,128]{1,0:T(8,128)S(1)} %bitcast.8), custom_call_target="tpu_custom_call" | custom-call | tf_op jit(solution)/shard_map/finish/pallas_call | solution.py:332

commit v8 on v7

--- a/solution.py
+++ b/solution.py
@@ -145,14 +145,6 @@
     operand = jnp.concatenate([high, high, low], 1)
     for copy in table_copies:
         copy.wait()
-    table = jnp.concatenate([table_ref[...], table_ref[:, :LANES]], 1)
-    values = lax.dot_general(
-        table, operand, (((1,), (1,)), ((), ())), preferred_element_type=jnp.float32
-    )
-    for parity in range(2):
-        part = values[:, parity * LANES : (parity + 1) * LANES]
-        out_ref[:, parity] = part.reshape(size, 2 * group, LANES)
-
     width = half * half
     exact = lax.Precision.HIGHEST
     spread = [jnp.concatenate([wave_ref[p]] * (cos_ref.shape[1] // LANES), 1) for p in range(2)]
@@ -173,12 +165,15 @@
         for parity in range(2):
             strip = strips[parity * half : (parity + 1) * half]
 
+            lanes = strip.shape[1]
+            turned = [
+                pltpu.roll(strip, lanes - shift, 1) if shift else strip
+                for shift in range(0, LANES, half)
+            ]
+
             def window(start):
                 base = start // LANES * LANES
-                part = strip[:, base : base + width + LANES]
-                if start > base:
-                    part = pltpu.roll(part, part.shape[1] - (start - base), 1)
-                return part[:, :width]
+                return turned[(start - base) // half][:, base : base + width]
 
             for x in range(half):
                 toeplitz = window((size - 1 - x) * half)
@@ -190,6 +185,14 @@
                     low_ref[c, parity, sign, x * half : (x + 1) * half, :] = low
 
     build(0, spectrum)
+
+    table = jnp.concatenate([table_ref[...], table_ref[:, :LANES]], 1)
+    values = lax.dot_general(
+        table, operand, (((1,), (1,)), ((), ())), preferred_element_type=jnp.float32
+    )
+    for parity in range(2):
+        part = values[:, parity * LANES : (parity + 1) * LANES]
+        out_ref[:, parity] = part.reshape(size, 2 * group, LANES)
 
     @pl.when(pair == 0)
     def _():
@@ -288,7 +291,7 @@
     high, low = split_table(spread.reshape(size * 2 * group, group * size))
     omega = math.pi / size
     freqs = np.arange(-(-(size + 1) // ROWS) * ROWS)
-    offsets = np.arange(-(size - 1), size + 1)
+    offsets = np.arange(-(size - 1), half + 1)
     angle = omega * np.outer(freqs, centred(size)[:half])
     waves = np.stack([np.cos(angle), np.sin(angle)])
     waves[0, size] = 0.0

time: 30.4 us -> 30.4 us (level)
  no operation moved by 1% of the time
where the time goes in v8:
time: 30.4 us; the launch traced here: 30.2 us
  blocking collectives  26 us (86%)
  Pallas kernels  4.13 us (14%)
    all_to_all x1, blocking collectives, tiled_program(): got = lax.all_to_all(components, AXES, 0, 0, tiled=True)  16.8 us
    all_to_all x1, blocking collectives, tiled_program(): parts = lax.all_to_all(rows, AXES, 0, 0, tiled=True)  9.24 us
    pallas_call x1, Pallas kernels, tiled_program(): pl.pallas_call(functools.partial(prepare_kernel, size, n_grid), out_shape...  2.79 us
    pallas_call x1, Pallas kernels, tiled_program(): pl.pallas_call(functools.partial(gram_kernel, n_vec, n_grid, group), out_...  0.67 us
    pallas_call x1, Pallas kernels, tiled_program(): pl.pallas_call(functools.partial(finish_kernel, n_vec), out_shape=jax.Sha...  0.67 us

profile of v8, /device:TPU:0, one launch (start us, length us, event | category | flops | bytes accessed | tf_op | source)
XLA Modules:
  0.0 30.2 jit_solution(7244818108245298601)
XLA Ops:
  0.0 2.8 %prepare.1 = (f32[32,2,8,128]{3,2,1,0:T(8,128)S(1)}, bf16[2,2,2,256,256]{4,3,2,1,0:T(8,128)(2,1)S(1)}, bf16[2,2,2,256,256]{4,3,2,1,0:T(8,128)(2,1)S(1)}) custom-call(f32[4,8,1024]{2,1,0:T(8,128)} %field_hbm.1, bf16[256,256]{1,0:T(8,128)(2,1)} %constant.8.clone.table_hbm, f32[40,768]{1,0:T(8,128)} %constant.9.clone.cos_hbm, ...), custom_call_target="tpu_custom_call" | custom-call | tf_op jit(solution)/shard_map/prepare/pallas_call | solution.py:308
  2.8 16.8 %all_to_all.16 = f32[32,2,8,128]{3,2,1,0:T(8,128)S(1)} all-to-all(f32[32,2,8,128]{3,2,1,0:T(8,128)S(1)} %get-tuple-element.8), channel_id=1, replica_groups=mesh['vec'=8,'grid'=4] {'vec','grid'}, dimensions={0} | all-to-all | bytes 524288 | tf_op jit(solution)/shard_map/all_to_all | solution.py:325
  19.6 0.7 %gram.1 = f32[32,128]{1,0:T(8,128)S(1)} custom-call(f32[512,128]{1,0:T(8,128)S(1)} %bitcast.6, bf16[2,2,2,256,256]{4,3,2,1,0:T(8,128)(2,1)S(1)} %get-tuple-element.9.high_ref, bf16[2,2,2,256,256]{4,3,2,1,0:T(8,128)(2,1)S(1)} %get-tuple-element.10.low_ref), custom_call_target="tpu_custom_call" | custom-call | tf_op jit(solution)/shard_map/gram/pallas_call | solution.py:326
  20.3 9.2 %all_to_all.17 = f32[32,1,128]{2,1,0:T(1,128)S(1)} all-to-all(f32[32,1,128]{2,1,0:T(1,128)S(1)} %bitcast.7), channel_id=1, replica_groups=mesh['vec'=8,'grid'=4] {'vec','grid'}, dimensions={0} | all-to-all | bytes 32768 | tf_op jit(solution)/shard_map/all_to_all | solution.py:334
  29.5 0.7 %finish.1 = f32[1,4,5]{2,1,0:T(4,128)} custom-call(f32[32,128]{1,0:T(8,128)S(1)} %bitcast.8), custom_call_target="tpu_custom_call" | custom-call | tf_op jit(solution)/shard_map/finish/pallas_call | solution.py:335

commit v9 on v8

--- a/solution.py
+++ b/solution.py
@@ -179,7 +179,7 @@
                 toeplitz = window((size - 1 - x) * half)
                 hankel = window(x * half)
                 for sign in range(2):
-                    value = 0.5 * (toeplitz - hankel if sign else toeplitz + hankel)
+                    value = toeplitz - hankel if sign else toeplitz + hankel
                     high, low = split_bf16(value)
                     high_ref[c, parity, sign, x * half : (x + 1) * half, :] = high
                     low_ref[c, parity, sign, x * half : (x + 1) * half, :] = low
@@ -296,7 +296,7 @@
     waves = np.stack([np.cos(angle), np.sin(angle)])
     waves[0, size] = 0.0
     waves[1, 0] = 0.0
-    turn = np.einsum("pky,pq->pyqk", waves, np.eye(2))
+    turn = np.einsum("pky,pq->pyqk", 0.5 * waves, np.eye(2))
     tables = [
         np.concatenate([high, low], 1),
         np.repeat(np.cos(omega * np.outer(freqs, offsets)), half, 1).astype(np.float32),

time: 30.4 us -> 30.3 us (level)
  no operation moved by 1% of the time
where the time goes in v9:
time: 30.3 us; the launch traced here: 30.2 us
  blocking collectives  26.1 us (86%)
  Pallas kernels  4.06 us (13%)
    all_to_all x1, blocking collectives, tiled_program(): got = lax.all_to_all(components, AXES, 0, 0, tiled=True)  16.8 us
    all_to_all x1, blocking collectives, tiled_program(): parts = lax.all_to_all(rows, AXES, 0, 0, tiled=True)  9.24 us
    pallas_call x1, Pallas kernels, tiled_program(): pl.pallas_call(functools.partial(prepare_kernel, size, n_grid), out_shape...  2.73 us
    pallas_call x1, Pallas kernels, tiled_program(): pl.pallas_call(functools.partial(gram_kernel, n_vec, n_grid, group), out_...  0.67 us
    pallas_call x1, Pallas kernels, tiled_program(): pl.pallas_call(functools.partial(finish_kernel, n_vec), out_shape=jax.Sha...  0.67 us

profile of v9, /device:TPU:0, one launch (start us, length us, event | category | flops | bytes accessed | tf_op | source)
XLA Modules:
  0.0 30.2 jit_solution(687164345272602116)
XLA Ops:
  0.0 2.7 %prepare.1 = (f32[32,2,8,128]{3,2,1,0:T(8,128)S(1)}, bf16[2,2,2,256,256]{4,3,2,1,0:T(8,128)(2,1)S(1)}, bf16[2,2,2,256,256]{4,3,2,1,0:T(8,128)(2,1)S(1)}) custom-call(f32[4,8,1024]{2,1,0:T(8,128)} %field_hbm.1, bf16[256,256]{1,0:T(8,128)(2,1)} %constant.8.clone.table_hbm, f32[40,768]{1,0:T(8,128)} %constant.9.clone.cos_hbm, ...), custom_call_target="tpu_custom_call" | custom-call | tf_op jit(solution)/shard_map/prepare/pallas_call | solution.py:308
  2.7 16.8 %all_to_all.16 = f32[32,2,8,128]{3,2,1,0:T(8,128)S(1)} all-to-all(f32[32,2,8,128]{3,2,1,0:T(8,128)S(1)} %get-tuple-element.8), channel_id=1, replica_groups=mesh['vec'=8,'grid'=4] {'vec','grid'}, dimensions={0} | all-to-all | bytes 524288 | tf_op jit(solution)/shard_map/all_to_all | solution.py:325
  19.6 0.7 %gram.1 = f32[32,128]{1,0:T(8,128)S(1)} custom-call(f32[512,128]{1,0:T(8,128)S(1)} %bitcast.6, bf16[2,2,2,256,256]{4,3,2,1,0:T(8,128)(2,1)S(1)} %get-tuple-element.9.high_ref, bf16[2,2,2,256,256]{4,3,2,1,0:T(8,128)(2,1)S(1)} %get-tuple-element.10.low_ref), custom_call_target="tpu_custom_call" | custom-call | tf_op jit(solution)/shard_map/gram/pallas_call | solution.py:326
  20.2 9.2 %all_to_all.17 = f32[32,1,128]{2,1,0:T(1,128)S(1)} all-to-all(f32[32,1,128]{2,1,0:T(1,128)S(1)} %bitcast.7), channel_id=1, replica_groups=mesh['vec'=8,'grid'=4] {'vec','grid'}, dimensions={0} | all-to-all | bytes 32768 | tf_op jit(solution)/shard_map/all_to_all | solution.py:334
  29.5 0.7 %finish.1 = f32[1,4,5]{2,1,0:T(4,128)} custom-call(f32[32,128]{1,0:T(8,128)S(1)} %bitcast.8), custom_call_target="tpu_custom_call" | custom-call | tf_op jit(solution)/shard_map/finish/pallas_call | solution.py:335

commit v10 on v8

--- a/solution.py
+++ b/solution.py
@@ -252,13 +252,13 @@
 
     first = (lax.axis_index("vec") == 0) & (lax.axis_index("grid") == 0)
 
+    @pl.when(jnp.logical_not(first))
+    def _():
+        gram_rows(True)
+
     @pl.when(first)
     def _():
         gram_rows(False)
-
-    @pl.when(jnp.logical_not(first))
-    def _():
-        gram_rows(True)
 
 
 def finish_kernel(n_vec, got_ref, out_ref):

time: 30.4 us -> 30.4 us (level)
  no operation moved by 1% of the time
where the time goes in v10:
time: 30.4 us; the launch traced here: 30.2 us
  blocking collectives  26 us (86%)
  Pallas kernels  4.13 us (14%)
    all_to_all x1, blocking collectives, tiled_program(): got = lax.all_to_all(components, AXES, 0, 0, tiled=True)  16.8 us
    all_to_all x1, blocking collectives, tiled_program(): parts = lax.all_to_all(rows, AXES, 0, 0, tiled=True)  9.24 us
    pallas_call x1, Pallas kernels, tiled_program(): pl.pallas_call(functools.partial(prepare_kernel, size, n_grid), out_shape...  2.79 us
    pallas_call x1, Pallas kernels, tiled_program(): pl.pallas_call(functools.partial(gram_kernel, n_vec, n_grid, group), out_...  0.67 us
    pallas_call x1, Pallas kernels, tiled_program(): pl.pallas_call(functools.partial(finish_kernel, n_vec), out_shape=jax.Sha...  0.67 us

profile of v10, /device:TPU:0, one launch (start us, length us, event | category | flops | bytes accessed | tf_op | source)
XLA Modules:
  0.0 30.2 jit_solution(7244818108245298601)
XLA Ops:
  0.0 2.8 %prepare.1 = (f32[32,2,8,128]{3,2,1,0:T(8,128)S(1)}, bf16[2,2,2,256,256]{4,3,2,1,0:T(8,128)(2,1)S(1)}, bf16[2,2,2,256,256]{4,3,2,1,0:T(8,128)(2,1)S(1)}) custom-call(f32[4,8,1024]{2,1,0:T(8,128)} %field_hbm.1, bf16[256,256]{1,0:T(8,128)(2,1)} %constant.8.clone.table_hbm, f32[40,768]{1,0:T(8,128)} %constant.9.clone.cos_hbm, ...), custom_call_target="tpu_custom_call" | custom-call | tf_op jit(solution)/shard_map/prepare/pallas_call | solution.py:308
  2.8 16.8 %all_to_all.16 = f32[32,2,8,128]{3,2,1,0:T(8,128)S(1)} all-to-all(f32[32,2,8,128]{3,2,1,0:T(8,128)S(1)} %get-tuple-element.8), channel_id=1, replica_groups=mesh['vec'=8,'grid'=4] {'vec','grid'}, dimensions={0} | all-to-all | bytes 524288 | tf_op jit(solution)/shard_map/all_to_all | solution.py:325
  19.6 0.7 %gram.1 = f32[32,128]{1,0:T(8,128)S(1)} custom-call(f32[512,128]{1,0:T(8,128)S(1)} %bitcast.6, bf16[2,2,2,256,256]{4,3,2,1,0:T(8,128)(2,1)S(1)} %get-tuple-element.9.high_ref, bf16[2,2,2,256,256]{4,3,2,1,0:T(8,128)(2,1)S(1)} %get-tuple-element.10.low_ref), custom_call_target="tpu_custom_call" | custom-call | tf_op jit(solution)/shard_map/gram/pallas_call | solution.py:326
  20.3 9.2 %all_to_all.17 = f32[32,1,128]{2,1,0:T(1,128)S(1)} all-to-all(f32[32,1,128]{2,1,0:T(1,128)S(1)} %bitcast.7), channel_id=1, replica_groups=mesh['vec'=8,'grid'=4] {'vec','grid'}, dimensions={0} | all-to-all | bytes 32768 | tf_op jit(solution)/shard_map/all_to_all | solution.py:334
  29.5 0.7 %finish.1 = f32[1,4,5]{2,1,0:T(4,128)} custom-call(f32[32,128]{1,0:T(8,128)S(1)} %bitcast.8), custom_call_target="tpu_custom_call" | custom-call | tf_op jit(solution)/shard_map/finish/pallas_call | solution.py:335
